TPU v7x, 32 devices: a whole 2x2x4 slice. The times are simulated.
32 devices in a mesh: comp: 4 (over x, core), tx: 4 (over z), ty: 2 (over y).
Axes of the slice: x: 2, y: 2, z: 4, core: 2. Of those that a mesh axis runs over, the one named last changes fastest.
Arguments:
- model_state: float32 [4, 4, 8, 512, 512], P('comp', None, None, 'tx', 'ty'), may hold values from -6 to 6
- sea_mask: int32 [4, 512, 512], P('comp', 'tx', 'ty'), may hold values 0 or 1
- wave_speed: float32 [4, 8], P('comp'), may hold values from 0.1 to 0.4
- diffusivity: float32 [4, 8], P('comp'), may hold values from 0.02 to 0.2
- surface_gains: float32 [4, 3], P('comp'), may hold values from 0.1 to 0.5
- area_table: float32 [256], replicated, may hold values from 0.2 to 1
- own_cells: int32 [4, 8, 4, 2048], P('comp', ('tx', 'ty')), may hold values from 0 to 32767
- target_cells: int32 [4, 8, 4, 2048], P('comp', ('tx', 'ty')), may hold values from 0 to 32767
- weight_ids: int32 [4, 8, 4, 2048], P('comp', ('tx', 'ty')), may hold values from 0 to 255
- pair_counts: int32 [4, 8, 4], P('comp', ('tx', 'ty')), may hold values from 512 to 2048, as said below
- fold_map: int32 [512], replicated, may hold values from 0 to 511, as said below
Outputs:
- new_state: float32 [4, 4, 8, 512, 512], P('comp', None, None, 'tx', 'ty')
Inputs may be any that keep to these rules, and one draw needn't show every extreme that they name: pair_counts[g, s, n] counts the live slots that position s of component g sends to its partner n; in every component one receiving position gets 2048 from each of the positions that have it as a partner. fold_map[fold_map[x]] == x.
All inputs are finite; a program needn't handle non-finite values. No bound on the sum of `sea_mask` on one device may be relied on, other than what follows from the above.
Results may differ from a plain program's by a relative error of at most 0.0001.
Values sent between devices are 32-bit elements; how exact they have to be, the bound alone decides.
No kernel may reach another device: no remote copies, remote signals or barrier semaphores. Data moves between devices by JAX's collectives and lax.ppermute only.
A program may use at most 192 MiB of HBM per device.

v0:
```python
import functools

import jax
import jax.numpy as jnp
import numpy
from jax import lax
from jax.experimental import pallas as pl
from jax.experimental.pallas import tpu as pltpu
from jax.sharding import PartitionSpec as P

LANES = 128
DEPTH = 8
PACKED = 16
VMEM_BYTES = 28 * 1024 * 1024
F32 = jnp.float32
BF16 = jnp.bfloat16
I32 = jnp.int32
CHANNELS = 5

EDGE_P, SECOND_P, EDGE_VELOCITY, EDGE_T, MASK = range(5)


def iota(shape, dim):
    return lax.broadcasted_iota(I32, shape, dim)


def halo_rows(levels):
    return (4 * levels + 1 + 7) // 8 * 8


def split_two(values):
    high = values.astype(BF16)
    low = (values - high.astype(F32)).astype(BF16)
    return high, low


def packed_ids(count):
    ids = iota((count, LANES), 0).astype(F32).astype(BF16)
    return ids.reshape(count // PACKED, PACKED, LANES)


def spread_row(row):
    return jnp.broadcast_to(row, (PACKED, LANES))


def share_bounds(slots, shares):
    bounds = [0]
    for m in range(shares):
        bounds.append(bounds[-1] + (slots - m + shares - 1) // shares)
    return bounds


def slot_order(slots, shares, sort, half):
    place = iota((8, LANES), 0) * LANES + iota((8, LANES), 1) + half * 8 * LANES
    source = jnp.zeros((8, LANES), I32)
    bounds = share_bounds(slots, shares)
    for m in range(shares):
        inside = jnp.logical_and(place >= bounds[m], place < bounds[m + 1])
        source = jnp.where(inside, (place - bounds[m]) * shares + m, source)
    return jnp.where(sort, source, place)


def pick_rows(ref, n, source):
    total = jnp.zeros((8, LANES), I32)
    for t in range(ref.shape[3] // LANES):
        row = jnp.broadcast_to(ref[0, 0, n : n + 1, t * LANES : (t + 1) * LANES], (8, LANES))
        picked = jnp.take_along_axis(row, source % LANES, axis=1)
        total = jnp.where(source // LANES == t, picked, total)
    return total


def prepare_partner(n, comps, refs, cells_ref, out):
    own_ref, target_ref, ids_ref, table_ref, counts_ref, picked_ref = refs
    slots = own_ref.shape[3]
    groups = slots // LANES
    is_ocean = lax.axis_index("comp") == comps - 1

    @pl.when(is_ocean)
    def _():
        for half in range(groups // 8):
            source = slot_order(slots, comps - 1, True, half)
            at = slice(half * 8, (half + 1) * 8)
            cells_ref[at, :] = pick_rows(own_ref, n, source)
            picked_ref[at, :] = pick_rows(ids_ref, n, source)
            out[4 * groups + half * 8 : 4 * groups + (half + 1) * 8, :] = pick_rows(target_ref, n, source).astype(F32)

    @pl.when(jnp.logical_not(is_ocean))
    def _():
        for g in range(groups):
            cut = slice(g * LANES, (g + 1) * LANES)
            cells_ref[g : g + 1, :] = own_ref[0, 0, n : n + 1, cut]
            picked_ref[g : g + 1, :] = ids_ref[0, 0, n : n + 1, cut]
            out[4 * groups + g : 4 * groups + g + 1, :] = target_ref[0, 0, n : n + 1, cut].astype(F32)

    count = jnp.broadcast_to(counts_ref[0, :, n : n + 1], (8, LANES))
    for half in range(groups // 8):
        source = slot_order(slots, comps - 1, is_ocean, half)
        ids = picked_ref[half * 8 : (half + 1) * 8, :]
        weight = jnp.zeros((8, LANES), F32)
        for t in range(table_ref.shape[0]):
            table = jnp.broadcast_to(table_ref[t : t + 1, :], (8, LANES))
            looked = jnp.take_along_axis(table, ids % LANES, axis=1)
            weight = jnp.where(ids // LANES == t, looked, weight)
        out[3 * groups + half * 8 : 3 * groups + (half + 1) * 8, :] = jnp.where(source < count, weight, 0.0)


def gather_partner(rows, cols, halves_ref, cells_ref, parts_ref, out):
    groups = cells_ref.shape[0]
    col_ids = packed_ids(cols)
    row_ids = iota((rows, LANES), 0)
    one = jnp.ones((), BF16)
    zero = jnp.zeros((), BF16)
    wide = 2
    subs = groups // wide

    def some(c, carry):
        for sub in range(subs):
            first = (c * subs + sub) * wide
            cells = [cells_ref[pl.ds(first + g, 1), :] for g in range(wide)]
            picks = []
            for cell in cells:
                col = spread_row(cell % cols).astype(F32).astype(BF16)
                picks.append(jnp.where(col_ids == col[None], one, zero).reshape(cols, LANES))
            picks = jnp.concatenate(picks, axis=1)
            if halves_ref.shape[1] > cols:
                picks = jnp.concatenate([picks, picks], axis=0)
                found = jnp.dot(halves_ref[...], picks, preferred_element_type=F32)
            else:
                found = jnp.dot(halves_ref[...], picks, preferred_element_type=F32)
                found = found[: 3 * rows] + found[3 * rows :]
            for g in range(wide):
                in_row = row_ids == cells[g] // cols
                for place, v in enumerate((2, 0, 1)):
                    block = found[v * rows : (v + 1) * rows, g * LANES : (g + 1) * LANES]
                    block = jnp.where(in_row, block, 0.0).reshape(rows // 8, 8, LANES)
                    start = pl.multiple_of((place * groups + first + g) * 8, 8)
                    parts_ref[pl.ds(start, 8), :] = jnp.sum(block, axis=0)
        return carry

    lax.fori_loop(0, groups // (subs * wide), some, 0)
    weight = out[3 * groups : 4 * groups, :]
    for place in range(3):
        total = jnp.zeros((groups, LANES), F32)
        for i in range(8):
            total += parts_ref[pl.ds(place * groups * 8 + i, groups, stride=8), :]
        out[place * groups : (place + 1) * groups, :] = total * weight


def split_surface(surface_ref, halves_ref, rows, cols):
    for v in range(3):
        high, low = split_two(surface_ref[v])
        if halves_ref.shape[1] > cols:
            halves_ref[v * rows : (v + 1) * rows, :cols] = high
            halves_ref[v * rows : (v + 1) * rows, cols:] = low
        else:
            halves_ref[v * rows : (v + 1) * rows, :] = high
            halves_ref[(v + 3) * rows : (v + 4) * rows, :] = low


def put_rows(ref, start, levels, cols, fields, sea, edge, second):
    height = halo_rows(levels)
    for p in range(cols // LANES):
        cut = slice(p * LANES, (p + 1) * LANES)
        base = start + p * height
        ref[base + 4 * levels : base + height, :] = jnp.zeros((height - 4 * levels, LANES), F32)
        ref[base + 4 * levels : base + 4 * levels + 1, :] = sea[edge : edge + 1, cut].astype(F32)
        for q, v, at in ((EDGE_P, 0, edge), (SECOND_P, 0, second), (EDGE_VELOCITY, 1, edge), (EDGE_T, 3, edge)):
            for l in range(levels):
                row = base + q * levels + l
                ref[row : row + 1, :] = fields(v, l)[at : at + 1, cut]


def turned_columns(levels, rows, fields, sea, begin):
    edge = 1 if begin else 0
    lanes = iota((rows, LANES), 1)
    total = pltpu.roll(sea.astype(F32), (4 * levels - begin - edge) % LANES, 1)
    for l in range(levels):
        total = jnp.where(lanes // 2 == l, pltpu.roll(fields(0, l), (2 * l - begin) % LANES, 1), total)
        for q, v in ((EDGE_VELOCITY, 2), (EDGE_T, 3)):
            at = q * levels + l
            moved = pltpu.roll(fields(v, l), (at - begin - edge) % LANES, 1)
            total = jnp.where(lanes == at, moved, total)
    return total.T[: halo_rows(levels)]


def first_body(
    levels, rows, cols, comps,
    state_hbm, own_hbm, target_hbm, ids_hbm, table_hbm, counts_hbm, mask_hbm,
    slab1_ref, up_ref, slab3_ref, fold_ref,
    surface_ref, own_ref, target_ref, ids_ref, table_ref, counts_ref, edge_ref, sea_edge_ref, mask_ref, columns_ref,
    halves_ref, cells_ref, picked_ref, parts_ref, copies, column_copies,
):
    sources = (
        own_hbm, target_hbm, ids_hbm, table_hbm, counts_hbm, state_hbm.at[0, pl.ds(1, 3), 0],
        state_hbm.at[0, :, :, pl.ds(rows - 8, 8), :], mask_hbm.at[0, pl.ds(rows - 8, 8), :],
    )
    places = (own_ref, target_ref, ids_ref, table_ref, counts_ref, surface_ref, edge_ref, sea_edge_ref)
    fetches = [
        pltpu.make_async_copy(source, place, copies.at[i])
        for i, (source, place) in enumerate(zip(sources, places))
    ]
    outer = pl.ds(cols - LANES, LANES)
    for_fold = [
        pltpu.make_async_copy(state_hbm.at[0, v, :, :, outer], columns_ref.at[i], column_copies.at[i])
        for i, v in enumerate((0, 2, 3))
    ] + [pltpu.make_async_copy(mask_hbm.at[0, :, outer], mask_ref, column_copies.at[3])]
    northern = lax.axis_index("ty") == lax.axis_size("ty") - 1
    folds = jnp.logical_and(lax.axis_index("comp") == comps - 1, northern)
    for fetch in fetches:
        fetch.start()

    @pl.when(folds)
    def _():
        for fetch in for_fold:
            fetch.start()

    for fetch in fetches[:5]:
        fetch.wait()
    refs = (own_ref, target_ref, ids_ref, table_ref, counts_ref, picked_ref)
    slabs = ((3, slab3_ref), (1, slab1_ref), (2, up_ref))
    for i, (n, out) in enumerate(slabs):
        prepare_partner(n, comps, refs, cells_ref.at[i], out)
    fetches[5].wait()
    split_surface(surface_ref, halves_ref, rows, cols)
    for i, (n, out) in enumerate(slabs):
        gather_partner(rows, cols, halves_ref, cells_ref.at[i], parts_ref, out)
    for fetch in fetches[6:]:
        fetch.wait()
    slab_rows = slab1_ref.shape[0]
    tall = halo_rows(levels) * (cols // LANES)
    put_rows(up_ref, slab_rows, levels, cols, lambda v, l: edge_ref.at[v, l], sea_edge_ref, 7, 6)

    @pl.when(folds)
    def _():
        for fetch in for_fold:
            fetch.wait()
        places = {0: 0, 2: 1, 3: 2}
        fold_ref[...] = turned_columns(
            levels, rows, lambda v, l: columns_ref[places[v], l], mask_ref[...], LANES - 2
        )

    @pl.when(jnp.logical_not(folds))
    def _():
        fold_ref[...] = jnp.zeros_like(fold_ref)

    up_ref[slab_rows + tall :, :] = fold_ref[...]
    slab3_ref[slab_rows:, :] = fold_ref[...]


def gather_scratch(rows, cols, slots, stacked):
    return [
        pltpu.VMEM((6 * rows, cols) if stacked else (3 * rows, 2 * cols), BF16),
        pltpu.VMEM((3, slots // LANES, LANES), I32),
        pltpu.VMEM((slots // LANES, LANES), I32),
        pltpu.VMEM((3 * slots // LANES * 8, LANES), F32),
    ]


def first_side(model_state, slot_arrays, sea_mask, comps):
    levels, rows, cols = model_state.shape[2:]
    near, slots = slot_arrays[0].shape[2:]
    table_shape = slot_arrays[3].shape
    slab = CHANNELS * slots // LANES
    height = halo_rows(levels)
    heights = (slab, slab + height * (cols // LANES) + height, slab + height, height)
    vmem = pl.BlockSpec(memory_space=pltpu.VMEM)
    arrays = (model_state, *slot_arrays, sea_mask)
    return pl.pallas_call(
        functools.partial(first_body, levels, rows, cols, comps),
        in_specs=[pl.BlockSpec(memory_space=pltpu.HBM)] * len(arrays),
        out_specs=[vmem] * len(heights),
        out_shape=[jax.ShapeDtypeStruct((h, LANES), F32) for h in heights],
        scratch_shapes=[pltpu.VMEM((3, rows, cols), F32)]
        + [pltpu.VMEM((1, 1, near, slots), I32)] * 3
        + [pltpu.VMEM(table_shape, F32), pltpu.VMEM((1, 1, near), I32)]
        + [
            pltpu.VMEM((4, levels, 8, cols), F32),
            pltpu.VMEM((8, cols), I32),
            pltpu.VMEM((rows, LANES), I32),
            pltpu.VMEM((3, levels, rows, LANES), F32),
        ]
        + gather_scratch(rows, cols, slots, True)
        + [pltpu.SemaphoreType.DMA((8,)), pltpu.SemaphoreType.DMA((4,))],
        compiler_params=pltpu.CompilerParams(vmem_limit_bytes=VMEM_BYTES),
    )(*(pltpu.with_memory_space_constraint(array, pltpu.HBM) for array in arrays))


def second_body(
    levels, rows, cols, comps, y_pair,
    state_ref, own_ref, target_ref, ids_ref, table_ref, counts_ref, fold_ref, mask_hbm,
    slab0_ref, down_ref, high_ref, low_ref, pair_ref, sent_ref,
    halves_ref, cells_ref, picked_ref, parts_ref, mask_ref, total_ref, copied,
):
    fetch = pltpu.make_async_copy(mask_hbm, mask_ref, copied)
    fetch.start()
    split_surface(state_ref.at[0, pl.ds(1, 3), 0], halves_ref, rows, cols)
    refs = (own_ref, target_ref, ids_ref, table_ref, counts_ref, picked_ref)
    prepare_partner(0, comps, refs, cells_ref.at[0], slab0_ref)
    gather_partner(rows, cols, halves_ref, cells_ref.at[0], parts_ref, slab0_ref)
    fetch.wait()
    put_rows(down_ref, 0, levels, cols, lambda v, l: state_ref.at[0, v, l], mask_ref.at[0], 0, 1)
    down_ref[halo_rows(levels) * (cols // LANES) :, :] = fold_ref[...]
    index_y = lax.axis_index("ty")
    high_used = index_y == 0 if y_pair else index_y >= 0
    low_used = index_y > 0 if y_pair else index_y >= 0

    def columns(start, begin):
        cut = slice(start, start + LANES)
        return turned_columns(levels, rows, lambda v, l: state_ref[0, v, l, :, cut], mask_ref[0, :, cut], begin)

    @pl.when(high_used)
    def _():
        highest = columns(cols - LANES, LANES - 2)
        high_ref[...] = highest
        pair_ref[...] = highest

    @pl.when(jnp.logical_not(high_used))
    def _():
        high_ref[...] = jnp.zeros_like(high_ref)

    @pl.when(low_used)
    def _():
        lowest = columns(0, 0)
        low_ref[...] = lowest
        pair_ref[...] = lowest

    @pl.when(jnp.logical_not(low_used))
    def _():
        low_ref[...] = jnp.zeros_like(low_ref)

    add_own(rows, cols, comps, own_ref.shape[3] // LANES, slab0_ref, total_ref, 0)
    sent_ref[...] = halves_added(total_ref, rows)


def second_side(model_state, slot_arrays, fold, sea_mask, comps, y_pair):
    levels, rows, cols = model_state.shape[2:]
    slots = slot_arrays[0].shape[3]
    height = halo_rows(levels)
    heights = (CHANNELS * slots // LANES, height * (cols // LANES) + height, height, height, height)
    vmem = pl.BlockSpec(memory_space=pltpu.VMEM)
    return pl.pallas_call(
        functools.partial(second_body, levels, rows, cols, comps, y_pair),
        in_specs=[vmem] * 7 + [pl.BlockSpec(memory_space=pltpu.HBM)],
        out_specs=[vmem] * (len(heights) + 1),
        out_shape=[jax.ShapeDtypeStruct((h, LANES), F32) for h in heights]
        + [jax.ShapeDtypeStruct((4 * rows, cols), F32)],
        scratch_shapes=gather_scratch(rows, cols, slots, False)
        + [pltpu.VMEM((1, rows, cols), I32), pltpu.VMEM((8 * rows, cols), F32), pltpu.SemaphoreType.DMA],
        compiler_params=pltpu.CompilerParams(vmem_limit_bytes=VMEM_BYTES),
    )(model_state, *slot_arrays, fold, pltpu.with_memory_space_constraint(sea_mask, pltpu.HBM))


def stencil_halos(
    levels, rows, cols, comps, count_x, count_y,
    state_ref, up_ref, down_ref, south_ref, north_ref, own_ref, fold_ref, far_refs, wave_ref, gains_ref,
    folded_ref, rows_ref, turned_ref,
):
    height = halo_rows(levels)
    parts = cols // LANES
    index_x = lax.axis_index("tx")
    index_y = lax.axis_index("ty")
    is_ocean = lax.axis_index("comp") == comps - 1
    last_y = index_y == count_y - 1
    has_west = jnp.where(jnp.logical_or(is_ocean, index_x > 0), 1.0, 0.0)
    has_east = jnp.where(jnp.logical_or(is_ocean, index_x < count_x - 1), 1.0, 0.0)
    has_south = jnp.where(index_y > 0, 1.0, 0.0)
    has_north = jnp.where(jnp.logical_or(is_ocean, jnp.logical_not(last_y)), 1.0, 0.0)
    drag = gains_ref[0, 2]
    mask_at = 4 * levels

    fold = fold_ref[pl.ds(index_x, 1), :]
    total = jnp.zeros((height, LANES), F32)
    up_start = up_ref.shape[0] - height * (parts + 1)
    sources = [(0, own_ref, 0), (-1, up_ref, up_start + height * parts), (1, down_ref, height * parts)]
    if north_ref.shape[0] > height:
        sources.append((2, north_ref, height))
    else:
        sources += [(shift, ref, 0) for shift, ref in zip(range(2, count_x - 1), far_refs)]
    for shift, ref, start in sources:
        at = lax.rem(index_x + shift + count_x, count_x)
        chosen = (iota((rows, rows), 0) + at * rows == fold).astype(F32)
        total += jnp.dot(
            ref[start : start + height, :], chosen,
            precision=lax.Precision.HIGHEST, preferred_element_type=F32,
        )
    folded_ref[...] = total

    line = iota((levels, LANES), 0)
    halves = jnp.zeros((levels, LANES), F32)
    for l in range(levels):
        halves = jnp.where(line == l, 0.5 * wave_ref[0, l], halves)

    def keeping(sea_values, drags):
        return jnp.where(is_ocean, sea_values, 1.0 - drags * (1.0 - sea_values))

    drags = jnp.where(line == 0, drag, 0.0)

    def by_level(ref, start, q):
        return ref[start + q * levels : start + (q + 1) * levels, :]

    for side, (ref, begin, sign, has) in enumerate(
        ((up_ref, up_start, 1.0, has_west), (down_ref, 0, -1.0, has_east))
    ):
        for p in range(parts):
            start = begin + p * height
            kept = keeping(ref[start + mask_at : start + mask_at + 1, :], drags)
            fixed = kept * (by_level(ref, start, EDGE_VELOCITY) + sign * halves * by_level(ref, start, SECOND_P))
            inner = rows - 1 if side else 0
            own = jnp.concatenate(
                [state_ref[0, 0, l, inner : inner + 1, p * LANES : (p + 1) * LANES] for l in range(levels)], axis=0
            )
            rows_ref[side, p, 0] = has * by_level(ref, start, EDGE_P)
            rows_ref[side, p, 1] = has * by_level(ref, start, EDGE_T)
            rows_ref[side, p, 2] = has * (fixed - sign * kept * halves * own)

    even = lambda ref: ref[pl.ds(0, levels, stride=2), :]
    odd = lambda ref: ref[pl.ds(1, levels, stride=2), :]
    north = [
        jnp.where(last_y, jnp.where(is_ocean, folded, 0.0), low)
        for folded, low in (
            (odd(folded_ref), even(north_ref)),
            (even(folded_ref), odd(north_ref)),
            (-by_level(folded_ref, 0, EDGE_VELOCITY), by_level(north_ref, 0, EDGE_VELOCITY)),
            (by_level(folded_ref, 0, EDGE_T), by_level(north_ref, 0, EDGE_T)),
            (folded_ref[mask_at : mask_at + 1, :], north_ref[mask_at : mask_at + 1, :]),
        )
    ]
    south = [
        odd(south_ref), even(south_ref), by_level(south_ref, 0, EDGE_VELOCITY), by_level(south_ref, 0, EDGE_T),
        south_ref[mask_at : mask_at + 1, :],
    ]
    fill = jnp.zeros((LANES // 2 - 4 * levels, LANES), F32)
    lines = []
    for (edge, second, velocity, tracer, sea), sign, has in (
        (south, 1.0, has_south), (north, -1.0, has_north)
    ):
        kept = keeping(sea, drags)
        fixed = has * kept * (velocity + sign * halves * second)
        lines += [has * edge, has * tracer, fixed, has * kept * halves, fill]
    high, low = split_two(jnp.concatenate(lines, axis=0).T)
    turned_ref[:, :LANES] = high
    turned_ref[:, LANES:] = low


def stencil_matrices(rows, cols):
    steps = [[numpy.eye(n, k=k, dtype=numpy.float32) for k in (1, -1, 0)] for n in (rows, cols)]
    after, before, _ = steps[0]
    along = [numpy.concatenate([m, m], axis=1) for m in (after - before, after + before)]
    before, after, centre = steps[1]
    across = [numpy.concatenate([m, m], axis=0) for m in (after - before, after + before - 4 * centre)]
    return jnp.asarray(numpy.stack(along), BF16), jnp.asarray(numpy.stack(across), BF16)


def stencil_levels(
    rows, cols, comps, begin, end, state_ref, mask_ref, rows_ref, turned_ref, wave_ref, spread_ref, gains_ref,
    along_ref, across_ref, place_refs, news_ref, after,
):
    levels = state_ref.shape[2]
    parts = cols // LANES
    is_ocean = lax.axis_index("comp") == comps - 1
    drag = gains_ref[0, 2]
    for ref in place_refs:
        ref[...] = jnp.zeros_like(ref)
    sea = mask_ref[0].astype(F32)
    tendency = jnp.where(is_ocean, sea, 1.0)
    first = iota((8, cols), 0) == 0
    last = iota((8, cols), 0) == 7
    places, lanes = iota((4 * levels, LANES), 0), iota((4 * levels, LANES), 1)

    def product(left, right):
        return jnp.dot(left, right, preferred_element_type=F32)

    def one_level(level, place_ref):
        half = 0.5 * wave_ref[0, level]
        spread = spread_ref[0, level]
        level_drag = jnp.where(level == 0, drag, 0.0)
        for q, sign in enumerate((-1.0, 1.0, -1.0, 1.0)):
            found = places == q * levels + level
            south = jnp.where(jnp.logical_and(found, lanes == 0), sign, 0.0).astype(BF16)
            north = jnp.where(jnp.logical_and(found, lanes == LANES - 1), 1.0, 0.0).astype(BF16)
            for term in range(2):
                at = term * LANES
                place_ref[q, at : at + 4 * levels, :LANES] = south
                at += LANES // 2
                place_ref[q, at : at + 4 * levels, cols - LANES :] = north

        def across(which, q, field):
            inner = product(jnp.concatenate(split_two(field), axis=1), across_ref[which])
            return inner + product(turned_ref[...], place_ref[q])

        def along(which, q, field):
            found = product(along_ref[which], jnp.concatenate(split_two(field), axis=0))
            west, east = (
                jnp.concatenate([rows_ref[side, p, q, pl.ds(level, 1), :] for p in range(parts)], axis=1)
                for side in range(2)
            )
            if which == 0:
                west = -west
            upper = found[:8] + jnp.where(first, west, 0.0)
            lower = found[rows - 8 :] + jnp.where(last, east, 0.0)
            return jnp.concatenate([upper, found[8 : rows - 8], lower], axis=0)

        pressure, zonal, meridional, tracer = (state_ref[0, v, level] for v in range(4))
        keep = jnp.where(is_ocean, sea, 1.0 - level_drag * (1.0 - sea))
        new_zonal = keep * (zonal - half * along(0, 0, pressure))
        new_meridional = keep * (meridional - half * across(0, 0, pressure))
        new_tracer = tracer + spread * tendency * (along(1, 1, tracer) + across(1, 1, tracer))
        beyond = product(turned_ref[...], place_ref[3]) * pressure
        divergence = along(0, 2, new_zonal) + across(0, 2, new_meridional) + beyond
        now = level - begin
        news_ref[0, now] = pressure - half * divergence
        news_ref[1, now] = new_zonal
        news_ref[2, now] = new_meridional
        news_ref[3, now] = new_tracer
        after(level)

    def some(c, carry):
        for i in range(length):
            one_level(begin + c * length + i, place_refs[i % len(place_refs)])
        return carry

    length = 4 if (end - begin) % 4 == 0 else 1
    lax.fori_loop(0, (end - begin) // length, some, 0)


def place_scratch(cols):
    return [pltpu.VMEM((4, 2 * LANES, cols), BF16)] * 2


def deep_body(
    sizes, begin,
    state_ref, mask_ref, up_ref, down_ref, south_ref, north_ref, own_ref, fold_ref,
    wave_ref, spread_ref, gains_ref, along_ref, across_ref, *rest,
):
    levels, rows, cols, comps, count_x, count_y = sizes
    far_refs, (news_ref, rows_ref, turned_ref, folded_ref, *place_refs) = rest[:-6], rest[-6:]
    stencil_halos(
        *sizes, state_ref, up_ref, down_ref, south_ref, north_ref, own_ref, fold_ref, far_refs, wave_ref, gains_ref,
        folded_ref, rows_ref, turned_ref,
    )
    stencil_levels(
        rows, cols, comps, begin, levels, state_ref, mask_ref, rows_ref, turned_ref, wave_ref, spread_ref, gains_ref,
        along_ref, across_ref, place_refs, news_ref, lambda level: None,
    )


def upper_body(
    sizes, end, begun_ref, state_ref, mask_ref, rows_ref, turned_ref, wave_ref, spread_ref, gains_ref,
    along_ref, across_ref, out_ref, new_surface_ref, old_surface_ref, place0, place1, news_ref, stores,
):
    levels, rows, cols, comps, count_x, count_y = sizes

    def store(l, v):
        return pltpu.make_async_copy(news_ref.at[v, l], out_ref.at[0, v, l], stores.at[l, v])

    def after(level):
        for v in range(4):
            store(level, v).start()

    stencil_levels(
        rows, cols, comps, 0, end, state_ref, mask_ref, rows_ref, turned_ref, wave_ref, spread_ref, gains_ref,
        along_ref, across_ref, (place0, place1), news_ref, after,
    )
    for v in range(3):
        new_surface_ref[v] = news_ref[v + 1, 0]
        old_surface_ref[v] = state_ref[0, v + 1, 0]
    for l in range(end):
        for v in range(4):
            store(l, v).wait()


def deep_levels(model_state, sea_mask, halos, fars, fold_map, wave_speed, diffusivity, gains, matrices, sizes, begin):
    levels, rows, cols, comps, count_x, count_y = sizes
    parts = cols // LANES
    fold = fold_map.reshape(count_x, rows)
    vmem = pl.BlockSpec(memory_space=pltpu.VMEM)
    scalar = pl.BlockSpec(memory_space=pltpu.SMEM)
    shapes = ((4, levels - begin, rows, cols), (2, parts, 3, levels, LANES), (rows, 2 * LANES))
    return pl.pallas_call(
        functools.partial(deep_body, sizes, begin),
        in_specs=[vmem] * 8 + [scalar] * 3 + [vmem] * (2 + len(fars)),
        out_specs=[vmem] * 3,
        out_shape=[jax.ShapeDtypeStruct(shape, kind) for shape, kind in zip(shapes, (F32, F32, BF16))],
        scratch_shapes=[
            pltpu.VMEM((halo_rows(levels), LANES), F32),
        ]
        + place_scratch(cols),
        compiler_params=pltpu.CompilerParams(vmem_limit_bytes=VMEM_BYTES),
    )(model_state, sea_mask, *halos, fold, wave_speed, diffusivity, gains, *matrices, *fars)


def upper_levels(
    begun, model_state, sea_mask, edge_rows, edge_columns, wave_speed, diffusivity, gains, matrices, sizes, end
):
    levels, rows, cols, comps, count_x, count_y = sizes
    vmem = pl.BlockSpec(memory_space=pltpu.VMEM)
    scalar = pl.BlockSpec(memory_space=pltpu.SMEM)
    anywhere = pl.BlockSpec(memory_space=pl.ANY)
    surface = jax.ShapeDtypeStruct((3, rows, cols), F32)
    return pl.pallas_call(
        functools.partial(upper_body, sizes, end),
        in_specs=[anywhere] + [vmem] * 4 + [scalar] * 3 + [vmem] * 2,
        out_specs=[anywhere, vmem, vmem],
        out_shape=[jax.ShapeDtypeStruct(begun.shape, F32), surface, surface],
        scratch_shapes=place_scratch(cols)
        + [pltpu.VMEM((4, end, rows, cols), F32), pltpu.SemaphoreType.DMA((end, 4))],
        input_output_aliases={0: 0},
        compiler_params=pltpu.CompilerParams(vmem_limit_bytes=VMEM_BYTES),
    )(begun, model_state, sea_mask, edge_rows, edge_columns, wave_speed, diffusivity, gains, *matrices)


def add_slots(rows, cols, groups, slab_ref, total_ref, chunks, plan, length, runs=1):
    row_ids = packed_ids(rows)
    col_ids = packed_ids(cols)
    lane = iota((1, LANES), 1)
    one = jnp.ones((), BF16)
    zero = jnp.zeros((), BF16)
    block = 4

    def one_chunk(total_ref, chunk):
        n, first, low_slot, high_slot = plan(chunk)
        start = n * (CHANNELS * groups) + first
        for begin in range(0, DEPTH, block):
            columns, spreads = [], []
            for g in range(begin, begin + block):
                cells = slab_ref[pl.ds(start + 4 * groups + g, 1), :].astype(I32)
                slot = lane + (first + g) * LANES
                mine = jnp.logical_and(slot >= low_slot, slot < high_slot)
                row = spread_row(jnp.where(mine, cells // cols, -1)).astype(F32).astype(BF16)
                col = spread_row(cells % cols).astype(F32).astype(BF16)
                columns.append(jnp.where(col_ids == col[None], one, zero).reshape(cols, LANES))
                in_row = row_ids == row[None]
                highs, lows = [], []
                for v in range(4):
                    value = spread_row(slab_ref[pl.ds(start + v * groups + g, 1), :])
                    high, low = split_two(value)
                    highs.append(jnp.where(in_row, high[None], zero).reshape(rows, LANES))
                    lows.append(jnp.where(in_row, low[None], zero).reshape(rows, LANES))
                spreads.append(jnp.concatenate(highs + lows, axis=0))
            total_ref[...] += lax.dot_general(
                jnp.concatenate(spreads, axis=1), jnp.concatenate(columns, axis=1), (((1,), (1,)), ((), ())),
                preferred_element_type=F32,
            )

    def turn(c, carry):
        for i in range(length):
            one_chunk(total_ref if runs == 1 else total_ref.at[c], c * length + i)
        return carry

    def single(c, carry):
        one_chunk(total_ref, c)
        return carry

    total_ref[...] = jnp.zeros_like(total_ref)
    turns = chunks // length
    lax.fori_loop(0, turns, turn, 0)
    if runs == 1:
        lax.fori_loop(turns * length, chunks, single, 0)


def halves_added(total_ref, rows):
    return total_ref[: 4 * rows] + total_ref[4 * rows :]


def add_own(rows, cols, comps, groups, slab_ref, total_ref, skipped):
    here = lax.axis_index("comp")
    pieces = groups // DEPTH
    near = slab_ref.shape[0] // (CHANNELS * groups) - skipped
    bounds = share_bounds(groups * LANES, comps - 1)
    is_ocean = here == comps - 1
    beside = here == comps - 2

    def plan(chunk):
        n = skipped + jnp.where(is_ocean, chunk, chunk // pieces)
        first = jnp.where(is_ocean, groups - DEPTH, chunk % pieces * DEPTH)
        return n, first, jnp.where(is_ocean, bounds[comps - 2], 0), groups * LANES

    chunks = jnp.where(is_ocean, near, jnp.where(beside, near * pieces, 0))
    add_slots(rows, cols, groups, slab_ref, total_ref, chunks, plan, 3 if near == 3 else 2)


def own_body(rows, cols, comps, groups, slab_ref, before_ref, sent_ref, total_ref):
    add_own(rows, cols, comps, groups, slab_ref, total_ref, 1)
    sent_ref[...] = before_ref[...] + halves_added(total_ref, rows)


def other_body(
    rows, cols, comps, groups, slab_ref, before_ref, deep_ref, kept_ref, sent_ref, state_ref,
    totals_ref, copies,
):
    here = lax.axis_index("comp")
    pieces = groups // DEPTH
    near = slab_ref.shape[0] // (CHANNELS * groups)
    bounds = share_bounds(groups * LANES, comps - 1)
    is_ocean = here == comps - 1
    beside = here == comps - 2
    for_two = here == comps - 3
    middle = bounds[1] // LANES // 4 * 4
    count = deep_ref.shape[1]
    stores = [
        pltpu.make_async_copy(
            deep_ref.at[v], state_ref.at[0, v, pl.ds(state_ref.shape[2] - count, count)], copies.at[v]
        )
        for v in range(4)
    ]
    for store in stores:
        store.start()

    def plan(chunk):
        mine = chunk >= near
        n = jnp.where(for_two, chunk % near, chunk // pieces)
        first = jnp.where(for_two, jnp.where(mine, middle, 0), chunk % pieces * DEPTH)
        low_slot = jnp.where(jnp.logical_and(for_two, mine), bounds[1], 0)
        high_slot = jnp.where(for_two, jnp.where(mine, bounds[2], bounds[1]), groups * LANES)
        return n, first, low_slot, high_slot

    chunks = jnp.where(here == 0, 0, near * pieces)
    add_slots(rows, cols, groups, slab_ref, totals_ref, chunks, plan, near * pieces // 2, 2)
    first_ref, second_ref = totals_ref.at[0], totals_ref.at[1]
    for start in range(0, 4 * rows, rows):
        first = first_ref[start : start + rows] + first_ref[start + 4 * rows : start + 5 * rows]
        second = second_ref[start : start + rows] + second_ref[start + 4 * rows : start + 5 * rows]
        kept_ref[start : start + rows] = jnp.where(beside, 0.0, second) + jnp.where(is_ocean, first, 0.0)
        sent = jnp.where(is_ocean, 0.0, first) + jnp.where(beside, second, 0.0)
        sent_ref[start : start + rows] = sent + before_ref[start : start + rows]
    for store in stores:
        store.wait()


def scatter_own(arrived, before, rows, cols, comps, slots):
    vmem = pl.BlockSpec(memory_space=pltpu.VMEM)
    return pl.pallas_call(
        functools.partial(own_body, rows, cols, comps, slots // LANES),
        in_specs=[vmem] * 2,
        out_specs=vmem,
        out_shape=jax.ShapeDtypeStruct((4 * rows, cols), F32),
        scratch_shapes=[pltpu.VMEM((8 * rows, cols), F32)],
        compiler_params=pltpu.CompilerParams(vmem_limit_bytes=VMEM_BYTES),
    )(arrived, before)


def scatter_other(other, before, deep, state_shape, rows, cols, comps, slots):
    vmem = pl.BlockSpec(memory_space=pltpu.VMEM)
    sums = jax.ShapeDtypeStruct((4 * rows, cols), F32)
    return pl.pallas_call(
        functools.partial(other_body, rows, cols, comps, slots // LANES),
        in_specs=[vmem] * 3,
        out_specs=[vmem, vmem, pl.BlockSpec(memory_space=pl.ANY)],
        out_shape=[sums, sums, jax.ShapeDtypeStruct(state_shape, F32)],
        scratch_shapes=[pltpu.VMEM((2, 8 * rows, cols), F32), pltpu.SemaphoreType.DMA((4,))],
        compiler_params=pltpu.CompilerParams(vmem_limit_bytes=VMEM_BYTES),
    )(other, before, deep)


def finish_body(rows, comps, state_ref, new_ref, old_ref, kept_ref, came_ref, mask_ref, gains_ref, out_ref, news_ref, copies):
    is_ocean = lax.axis_index("comp") == comps - 1
    tendency = jnp.where(is_ocean, mask_ref[0].astype(F32), 1.0)
    sums = [kept_ref[v * rows : (v + 1) * rows, :] + came_ref[v * rows : (v + 1) * rows, :] for v in range(4)]
    saves = []
    for v, total, gain in ((0, sums[1], 1), (1, sums[2], 1), (2, sums[0], 0)):
        news_ref[v] = new_ref[v] + tendency * gains_ref[0, gain] * (total - sums[3] * old_ref[v])
        saves.append(pltpu.make_async_copy(news_ref.at[v], out_ref.at[0, v + 1, 0], copies.at[v]))
        saves[-1].start()
    for save in saves:
        save.wait()


def finish(state, new_surface, old_surface, kept, came, sea_mask, gains, comps):
    rows, cols = state.shape[3:]
    vmem = pl.BlockSpec(memory_space=pltpu.VMEM)
    anywhere = pl.BlockSpec(memory_space=pl.ANY)
    return pl.pallas_call(
        functools.partial(finish_body, rows, comps),
        in_specs=[anywhere] + [vmem] * 5 + [pl.BlockSpec(memory_space=pltpu.SMEM)],
        out_specs=anywhere,
        out_shape=jax.ShapeDtypeStruct(state.shape, F32),
        scratch_shapes=[pltpu.VMEM((3, rows, cols), F32), pltpu.SemaphoreType.DMA((3,))],
        input_output_aliases={0: 0},
        compiler_params=pltpu.CompilerParams(vmem_limit_bytes=VMEM_BYTES),
    )(state, new_surface, old_surface, kept, came, sea_mask, gains)


def shards(
    model_state, sea_mask, wave_speed, diffusivity, surface_gains, area_table,
    own_cells, target_cells, weight_ids, pair_counts, fold_map,
):
    comps, count_x, count_y = (lax.axis_size(a) for a in ("comp", "tx", "ty"))
    positions = count_x * count_y
    rows, cols = model_state.shape[3:]
    slots = own_cells.shape[3]
    slot_arrays = (own_cells, target_cells, weight_ids, area_table.reshape(-1, LANES), pair_counts)

    def along(block, shift):
        return lax.ppermute(block, ("tx", "ty"), [(s, (s + shift) % positions) for s in range(positions)])

    y_pair = count_y == 2
    slab_rows = CHANNELS * slots // LANES
    slab1, up, slab3, fold = first_side(model_state, slot_arrays, sea_mask, comps)
    slab3 = along(slab3, 1 + count_y)
    slab1 = along(slab1, 1)
    up = along(up, count_y)
    slab0, down, high, low, pair, before = second_side(model_state, slot_arrays, fold, sea_mask, comps, y_pair)
    arrived = jnp.concatenate([slab0, slab1, up[:slab_rows], slab3[:slab_rows]])
    down = along(down, -count_y)
    fars = []
    if y_pair and count_x == 4:
        south = north = lax.ppermute(jnp.concatenate([pair, slab3[slab_rows:]]), "ty", [(0, 1), (1, 0)])
    else:
        south = lax.ppermute(high, "ty", [(j, j + 1) for j in range(count_y - 1)])
        north = lax.ppermute(low, "ty", [(j + 1, j) for j in range(count_y - 1)])
        for shift in range(2, count_x - 1):
            pairs = []
            for i in range(count_x):
                ends = [((comps - 1) * count_x + k) * count_y + count_y - 1 for k in ((i + shift) % count_x, i)]
                pairs.append(tuple(ends))
            fars.append(lax.ppermute(fold, ("comp", "tx", "ty"), pairs))

    other = lax.ppermute(arrived, "comp", [(g, g ^ 2) for g in range(comps)])

    sizes = (*model_state.shape[2:], comps, count_x, count_y)
    cut = sizes[0] // 2
    matrices = stencil_matrices(rows, cols)
    before = scatter_own(arrived, before, rows, cols, comps, slots)
    deep, edge_rows, edge_columns = deep_levels(
        model_state, sea_mask, (up, down, south, north, fold), fars, fold_map,
        wave_speed, diffusivity, surface_gains, matrices, sizes, cut,
    )
    kept, sent, begun = scatter_other(other, before, deep, model_state.shape, rows, cols, comps, slots)
    came = lax.ppermute(sent, "comp", [(g, g ^ 1) for g in range(comps)])
    new_state, new_surface, old_surface = upper_levels(
        begun, model_state, sea_mask, edge_rows, edge_columns, wave_speed, diffusivity, surface_gains,
        matrices, sizes, cut,
    )
    return finish(new_state, new_surface, old_surface, kept, came, sea_mask, surface_gains, comps)


def solution(mesh):
    in_specs = (
        P("comp", None, None, "tx", "ty"),
        P("comp", "tx", "ty"),
        P("comp", None),
        P("comp", None),
        P("comp", None),
        P(),
        P("comp", ("tx", "ty"), None, None),
        P("comp", ("tx", "ty"), None, None),
        P("comp", ("tx", "ty"), None, None),
        P("comp", ("tx", "ty"), None),
        P(),
    )
    out_specs = P("comp", None, None, "tx", "ty")
    return jax.shard_map(shards, mesh=mesh, in_specs=in_specs, out_specs=out_specs, check_vma=False)
```

profile of v0, /device:TPU:3, one launch (start us, length us, event | category | flops | bytes accessed | tf_op | source)
XLA Modules:
  0.0 35.2 jit_solution(13621609053559899999)
XLA Ops:
  0.0 0.0 copy-start
  0.0 0.0 copy-start.10
  0.0 0.0 copy-start.6
  0.0 0.0 copy-start.5
  0.0 0.0 copy-start.4
  0.0 0.0 copy-start.8
  0.0 4.8 %shard_map.127 = (f32[80,128]{1,0:T(8,128)S(1)}, f32[200,128]{1,0:T(8,128)S(1)}, f32[120,128]{1,0:T(8,128)S(1)}, f32[40,128]{1,0:T(8,128)S(1)}) custom-call(f32[1,4,8,128,256]{4,3,2,1,0:T(8,128)} %state_ref.5, s32[1,1,4,2048]{3,2,1,0:T(4,128)} %own_ref.1, s32[1,1,4,2048]{3,2,1,0:T(4,128)} %target_ref.1, s32[1,1,4,2048]{3,2,1,0:T(4,128)} %ids_ref.1, ...), custom_call_target="tpu_custom_call" | custom-call | tf_op jit(solution)/shard_map/pallas_call | solution.py:268
  4.8 0.0 copy-start.1
  4.9 0.0 copy-start.2
  4.9 0.0 copy-start.3
  4.9 0.0 copy-start.7
  4.9 0.0 copy-start.9
  4.9 0.0 copy-start.11
  4.9 0.0 copy-start.12
  4.9 1.3 %collective-permute-start.1 = (f32[200,128]{1,0:T(8,128)S(1)}, f32[200,128]{1,0:T(8,128)S(1)}, u32[]{:S(2)}, u32[]{:S(2)}) collective-permute-start(f32[200,128]{1,0:T(8,128)S(1)} %get-tuple-element.25), channel_id=1, source_target_pairs={{0,2},{1,3},{2,4},{3,5},{4,6},{5,7},{6,0},{7,1},{8,10},{9,11},{10,... | collective-permute-start | bytes 307208 | tf_op jit(solution)/shard_map/ppermute | solution.py:794
  6.3 2.8 %collective-permute-start.2 = (f32[120,128]{1,0:T(8,128)S(1)}, f32[120,128]{1,0:T(8,128)S(1)}, u32[]{:S(2)}, u32[]{:S(2)}) collective-permute-start(f32[120,128]{1,0:T(8,128)S(1)} %get-tuple-element.26), channel_id=1, source_target_pairs={{0,3},{1,4},{2,5},{3,6},{4,7},{5,0},{6,1},{7,2},{8,11},{9,12},{10,... | collective-permute-start | bytes 184328 | tf_op jit(solution)/shard_map/ppermute | solution.py:794
  9.1 0.7 %collective-permute-start = (f32[80,128]{1,0:T(8,128)S(1)}, f32[80,128]{1,0:T(8,128)S(1)}, u32[]{:S(2)}, u32[]{:S(2)}) collective-permute-start(f32[80,128]{1,0:T(8,128)S(1)} %get-tuple-element.24), channel_id=1, source_target_pairs={{0,1},{1,2},{2,3},{3,4},{4,5},{5,6},{6,7},{7,0},{8,9},{9,10},{10,1... | collective-permute-start | bytes 122888 | tf_op jit(solution)/shard_map/ppermute | solution.py:794
  9.8 0.0 copy-done
  9.8 0.0 copy-done.10
  9.8 0.0 copy-done.6
  9.8 0.0 copy-done.5
  9.8 0.0 copy-done.4
  9.8 0.0 copy-done.8
  9.8 3.3 %shard_map.128 = (f32[80,128]{1,0:T(8,128)S(1)}, f32[120,128]{1,0:T(8,128)S(1)}, f32[40,128]{1,0:T(8,128)}, f32[40,128]{1,0:T(8,128)}, f32[40,128]{1,0:T(8,128)S(1)}, /*index=5*/f32[512,256]{1,0:T(8,128)S(1)}) custom-call(f32[1,4,8,128,256]{4,3,2,1,0:T(8,128)S(1)} %copy-done, s32[1,1,4,2048]{3,2,1,0:T(4,128)S(1)} %copy-done.4, ...), custom_call_target="tpu_custom_call" | custom-call | tf_op jit(solution)/shard_map/pallas_call | solution.py:341
  13.2 3.6 %collective-permute-done.2 = f32[120,128]{1,0:T(8,128)S(1)} collective-permute-done((f32[120,128]{1,0:T(8,128)S(1)}, f32[120,128]{1,0:T(8,128)S(1)}, u32[]{:S(2)}, u32[]{:S(2)}) %collective-permute-start.2) | collective-permute-done | bytes 61472 | tf_op jit(solution)/shard_map/ppermute | solution.py:794
  16.7 0.0 collective-permute-done.1.up_ref
  16.7 0.0 collective-permute-done
  16.8 0.1 collective-permute-start.3
  16.8 0.4 %collective-permute-start.4 = (f32[120,128]{1,0:T(8,128)S(1)}, f32[120,128]{1,0:T(8,128)S(1)}, u32[]{:S(2)}, u32[]{:S(2)}) collective-permute-start(f32[120,128]{1,0:T(8,128)S(1)} %get-tuple-element.28), channel_id=1, source_target_pairs={{0,6},{1,7},{2,0},{3,1},{4,2},{5,3},{6,4},{7,5},{8,14},{9,15},{10,... | collective-permute-start | bytes 184328 | tf_op jit(solution)/shard_map/ppermute | solution.py:794
  17.2 0.0 collective-permute-start.5
  17.3 2.2 %shard_map.129.before_ref = f32[512,256]{1,0:T(8,128)S(1)} custom-call(f32[320,128]{1,0:T(8,128)S(1)} %pad_maximum_fusion.slab_ref, f32[512,256]{1,0:T(8,128)S(1)} %get-tuple-element.27.before_ref), custom_call_target="tpu_custom_call" | custom-call | tf_op jit(solution)/shard_map/pallas_call | solution.py:732
  19.5 0.5 %collective-permute-done.4.down_ref = f32[120,128]{1,0:T(8,128)S(1)} collective-permute-done((f32[120,128]{1,0:T(8,128)S(1)}, f32[120,128]{1,0:T(8,128)S(1)}, u32[]{:S(2)}, u32[]{:S(2)}) %collective-permute-start.4) | collective-permute-done | bytes 61472 | tf_op jit(solution)/shard_map/ppermute | solution.py:794
  20.0 0.1 collective-permute-done.5.south_ref.north_ref
  20.1 0.0 copy-done.1
  20.1 0.0 copy-done.2
  20.1 0.0 copy-done.3
  20.1 0.0 copy-done.7
  20.1 0.0 copy-done.9
  20.1 0.0 copy-done.11
  20.1 0.0 copy-done.12
  20.2 2.7 %shard_map.130 = (f32[4,4,128,256]{3,2,1,0:T(8,128)S(1)}, f32[2,2,3,8,128]{4,3,2,1,0:T(8,128)S(1)}, bf16[128,256]{1,0:T(8,128)(2,1)S(1)}) custom-call(f32[1,4,8,128,256]{4,3,2,1,0:T(8,128)S(1)} %copy-done, s32[1,128,256]{2,1,0:T(8,128)S(1)} %copy-done.1, f32[200,128]{1,0:T(8,128)S(1)} %collective-permute-done.1.up_ref, ...), custom_call_target="tpu_custom_call" | custom-call | tf_op jit(solution)/shard_map/pallas_call | solution.py:579
  22.9 0.0 collective-permute-done.3.slab_ref
  22.9 5.2 %shard_map.131 = (f32[512,256]{1,0:T(8,128)S(1)}, f32[512,256]{1,0:T(8,128)S(1)}, f32[1,4,8,128,256]{4,3,2,1,0:T(8,128)}) custom-call(f32[320,128]{1,0:T(8,128)S(1)} %collective-permute-done.3.slab_ref, f32[512,256]{1,0:T(8,128)S(1)} %shard_map.129.before_ref, f32[4,4,128,256]{3,2,1,0:T(8,128)S(1)} %get-tuple-element.30.deep_ref), custom_call_target="tpu_custom_call" | custom-call | tf_op jit(solution)/shard_map/pallas_call | solution.py:745
  28.0 2.6 %collective-permute-start.6 = (f32[512,256]{1,0:T(8,128)S(1)}, f32[512,256]{1,0:T(8,128)S(1)}, u32[]{:S(2)}, u32[]{:S(2)}) collective-permute-start(f32[512,256]{1,0:T(8,128)S(1)} %get-tuple-element.38), channel_id=1, source_target_pairs={{0,8},{8,0},{16,24},{24,16},{1,9},{9,1},{17,25},{25,17},{2,10},{10... | collective-permute-start | bytes 1572872 | tf_op jit(solution)/shard_map/ppermute | solution.py:829
  30.7 3.0 %shard_map.132 = (f32[1,4,8,128,256]{4,3,2,1,0:T(8,128)}, f32[3,128,256]{2,1,0:T(8,128)S(1)}, f32[3,128,256]{2,1,0:T(8,128)S(1)}) custom-call(f32[1,4,8,128,256]{4,3,2,1,0:T(8,128)} %get-tuple-element.31.begun_ref, f32[1,4,8,128,256]{4,3,2,1,0:T(8,128)S(1)} %copy-done, s32[1,128,256]{2,1,0:T(8,128)S(1)} %copy-done.1, ...), custom_call_target="tpu_custom_call", output_to_operand_aliasing={{0}: (0, {})} | custom-call | tf_op jit(solution)/shard_map/pallas_call | solution.py:600
  33.7 0.0 collective-permute-done.6.came_ref
  33.7 1.4 %shard_map.133 = f32[1,4,8,128,256]{4,3,2,1,0:T(8,128)} custom-call(f32[1,4,8,128,256]{4,3,2,1,0:T(8,128)} %get-tuple-element.34.state_ref, f32[3,128,256]{2,1,0:T(8,128)S(1)} %get-tuple-element.35.new_ref, f32[3,128,256]{2,1,0:T(8,128)S(1)} %get-tuple-element.36.old_ref, f32[512,256]{1,0:T(8,128)S(1)} %get-tuple-element.37.kept_ref, ...), custom_call_target="tpu_custom_call", output_to_operand_aliasing={{}: (0, {})} | custom-call | tf_op jit(solution)/shard_map/pallas_call | solution.py:772
  (5 shorter events, 0.0 us)
Async XLA Ops:
  0.0 9.8 %copy-start = (f32[1,4,8,128,256]{4,3,2,1,0:T(8,128)S(1)}, f32[1,4,8,128,256]{4,3,2,1,0:T(8,128)}, u32[]{:S(2)}) copy-start(f32[1,4,8,128,256]{4,3,2,1,0:T(8,128)} %state_ref.5) | copy-start | bytes 12582916
  0.0 9.8 %copy-start.10 = (s32[1,1,4]{2,1,0:T(1,128)S(1)}, s32[1,1,4]{2,1,0:T(1,128)}, u32[]{:S(2)}) copy-start(s32[1,1,4]{2,1,0:T(1,128)} %counts_ref.1) | copy-start | bytes 52
  0.0 9.8 %copy-start.6 = (s32[1,1,4,2048]{3,2,1,0:T(4,128)S(1)}, s32[1,1,4,2048]{3,2,1,0:T(4,128)}, u32[]{:S(2)}) copy-start(s32[1,1,4,2048]{3,2,1,0:T(4,128)} %ids_ref.1) | copy-start | bytes 98308
  0.0 9.8 %copy-start.5 = (s32[1,1,4,2048]{3,2,1,0:T(4,128)S(1)}, s32[1,1,4,2048]{3,2,1,0:T(4,128)}, u32[]{:S(2)}) copy-start(s32[1,1,4,2048]{3,2,1,0:T(4,128)} %target_ref.1) | copy-start | bytes 98308
  0.0 9.8 %copy-start.4 = (s32[1,1,4,2048]{3,2,1,0:T(4,128)S(1)}, s32[1,1,4,2048]{3,2,1,0:T(4,128)}, u32[]{:S(2)}) copy-start(s32[1,1,4,2048]{3,2,1,0:T(4,128)} %own_ref.1) | copy-start | bytes 98308
  0.0 9.8 %copy-start.8 = (f32[256]{0:T(256)S(1)}, f32[256]{0:T(256)}, u32[]{:S(2)}) copy-start(f32[256]{0:T(256)} %param.18) | copy-start | bytes 3076
  4.8 15.3 %copy-start.1 = (s32[1,128,256]{2,1,0:T(8,128)S(1)}, s32[1,128,256]{2,1,0:T(8,128)}, u32[]{:S(2)}) copy-start(s32[1,128,256]{2,1,0:T(8,128)} %mask_ref.5) | copy-start | bytes 393220
  4.9 15.3 %copy-start.2 = (bf16[2,512,256]{2,1,0:T(8,128)(2,1)S(1)}, bf16[2,512,256]{2,1,0:T(8,128)(2,1)}, u32[]{:S(2)}) copy-start(bf16[2,512,256]{2,1,0:T(8,128)(2,1)} %constant.5.clone.across_ref) | copy-start | bytes 1572868
  4.9 15.2 %copy-start.3 = (bf16[2,128,256]{2,1,0:T(8,128)(2,1)S(1)}, bf16[2,128,256]{2,1,0:T(8,128)(2,1)}, u32[]{:S(2)}) copy-start(bf16[2,128,256]{2,1,0:T(8,128)(2,1)} %constant.4.clone.along_ref) | copy-start | bytes 393220
  4.9 15.2 %copy-start.7 = (f32[1,3]{1,0:T(1,128)S(1)}, f32[1,3]{1,0:T(1,128)}, u32[]{:S(2)}) copy-start(f32[1,3]{1,0:T(1,128)} %gains_ref.5) | copy-start | bytes 40
  4.9 15.2 %copy-start.9 = (s32[512]{0:T(512)S(1)}, s32[512]{0:T(512)}, u32[]{:S(2)}) copy-start(s32[512]{0:T(512)} %param.23) | copy-start | bytes 6148
  4.9 15.2 %copy-start.11 = (f32[1,8]{1,0:T(1,128)S(1)}, f32[1,8]{1,0:T(1,128)}, u32[]{:S(2)}) copy-start(f32[1,8]{1,0:T(1,128)} %wave_ref.3) | copy-start | bytes 100
  4.9 15.2 %copy-start.12 = (f32[1,8]{1,0:T(1,128)S(1)}, f32[1,8]{1,0:T(1,128)}, u32[]{:S(2)}) copy-start(f32[1,8]{1,0:T(1,128)} %spread_ref.3) | copy-start | bytes 100
  4.9 11.8 %collective-permute-start.1 = (f32[200,128]{1,0:T(8,128)S(1)}, f32[200,128]{1,0:T(8,128)S(1)}, u32[]{:S(2)}, u32[]{:S(2)}) collective-permute-start(f32[200,128]{1,0:T(8,128)S(1)} %get-tuple-element.25), channel_id=1, source_target_pairs={{0,2},{1,3},{2,4},{3,5},{4,6},{5,7},{6,0},{7,1},{8,10},{9,11},{10,... | collective-permute-start | bytes 307208 | tf_op jit(solution)/shard_map/ppermute | solution.py:794
  6.3 10.4 %collective-permute-start.2 = (f32[120,128]{1,0:T(8,128)S(1)}, f32[120,128]{1,0:T(8,128)S(1)}, u32[]{:S(2)}, u32[]{:S(2)}) collective-permute-start(f32[120,128]{1,0:T(8,128)S(1)} %get-tuple-element.26), channel_id=1, source_target_pairs={{0,3},{1,4},{2,5},{3,6},{4,7},{5,0},{6,1},{7,2},{8,11},{9,12},{10,... | collective-permute-start | bytes 184328 | tf_op jit(solution)/shard_map/ppermute | solution.py:794
  9.1 7.7 %collective-permute-start = (f32[80,128]{1,0:T(8,128)S(1)}, f32[80,128]{1,0:T(8,128)S(1)}, u32[]{:S(2)}, u32[]{:S(2)}) collective-permute-start(f32[80,128]{1,0:T(8,128)S(1)} %get-tuple-element.24), channel_id=1, source_target_pairs={{0,1},{1,2},{2,3},{3,4},{4,5},{5,6},{6,7},{7,0},{8,9},{9,10},{10,1... | collective-permute-start | bytes 122888 | tf_op jit(solution)/shard_map/ppermute | solution.py:794
  16.8 6.1 %collective-permute-start.3 = (f32[320,128]{1,0:T(8,128)S(1)}, f32[320,128]{1,0:T(8,128)S(1)}, u32[]{:S(2)}, u32[]{:S(2)}) collective-permute-start(f32[320,128]{1,0:T(8,128)S(1)} %pad_maximum_fusion.slab_ref), channel_id=1, source_target_pairs={{0,16},{8,24},{16,0},{24,8},{1,17},{9,25},{17,1},{25,9},{2,18},{10... | collective-permute-start | bytes 491528 | tf_op jit(solution)/shard_map/ppermute | solution.py:818
  16.8 3.1 %collective-permute-start.4 = (f32[120,128]{1,0:T(8,128)S(1)}, f32[120,128]{1,0:T(8,128)S(1)}, u32[]{:S(2)}, u32[]{:S(2)}) collective-permute-start(f32[120,128]{1,0:T(8,128)S(1)} %get-tuple-element.28), channel_id=1, source_target_pairs={{0,6},{1,7},{2,0},{3,1},{4,2},{5,3},{6,4},{7,5},{8,14},{9,15},{10,... | collective-permute-start | bytes 184328 | tf_op jit(solution)/shard_map/ppermute | solution.py:794
  17.2 2.9 %collective-permute-start.5 = (f32[80,128]{1,0:T(8,128)S(1)}, f32[80,128]{1,0:T(8,128)S(1)}, u32[]{:S(2)}, u32[]{:S(2)}) collective-permute-start(f32[80,128]{1,0:T(8,128)S(1)} %pad_maximum_fusion.1), channel_id=1, source_target_pairs={{0,1},{1,0},{2,3},{3,2},{4,5},{5,4},{6,7},{7,6},{8,9},{9,8},{10,11... | collective-permute-start | bytes 122888 | tf_op jit(solution)/shard_map/ppermute | solution.py:807
  28.0 5.7 %collective-permute-start.6 = (f32[512,256]{1,0:T(8,128)S(1)}, f32[512,256]{1,0:T(8,128)S(1)}, u32[]{:S(2)}, u32[]{:S(2)}) collective-permute-start(f32[512,256]{1,0:T(8,128)S(1)} %get-tuple-element.38), channel_id=1, source_target_pairs={{0,8},{8,0},{16,24},{24,16},{1,9},{9,1},{17,25},{25,17},{2,10},{10... | collective-permute-start | bytes 1572872 | tf_op jit(solution)/shard_map/ppermute | solution.py:829
where the time goes:
time: 35.6 us; the launch traced here: 35.2 us
  Pallas kernels  22.6 us (63%)
  starting transfers between devices  7.96 us (22%)
  waiting for transfers between devices  4.19 us (12%)
  between operations  0.4 us (1%)
    ppermute x4, starting transfers between devices, along(): lax.ppermute(block, ('tx', 'ty'), [(s, (s + shift) % positions) for s in...  5.24 us
    pallas_call x1, Pallas kernels, scatter_other(): pl.pallas_call(functools.partial(other_body, rows, cols, comps, slots //...  5.16 us
    pallas_call x1, Pallas kernels, first_side(): pl.pallas_call(functools.partial(first_body, levels, rows, cols, comps),...  4.8 us
    ppermute x4, waiting for transfers between devices, along(): lax.ppermute(block, ('tx', 'ty'), [(s, (s + shift) % positions) for s in...  4.05 us
    pallas_call x1, Pallas kernels, second_side(): pl.pallas_call(functools.partial(second_body, levels, rows, cols, comps,...  3.34 us
    pallas_call x1, Pallas kernels, upper_levels(): pl.pallas_call(functools.partial(upper_body, sizes, end), in_specs=[anywh...  3.01 us
    pallas_call x1, Pallas kernels, deep_levels(): pl.pallas_call(functools.partial(deep_body, sizes, begin), in_specs=[vmem...  2.69 us
    ppermute x1, starting transfers between devices, shards(): came = lax.ppermute(sent, 'comp', [(g, g ^ 1) for g in range(comps)])  2.64 us
  transfers between devices with their start and end apart: 7, of which 3 were waited for; matrix products, arithmetic and copies ran while one was open for 0% of the time, Pallas kernels for 32%

commit v1 on v0

--- a/solution.py
+++ b/solution.py
@@ -519,7 +519,7 @@
             one_level(begin + c * length + i, place_refs[i % len(place_refs)])
         return carry
 
-    length = 4 if (end - begin) % 4 == 0 else 1
+    length = 2 if (end - begin) % 2 == 0 else 1
     lax.fori_loop(0, (end - begin) // length, some, 0)
 
 
@@ -680,7 +680,7 @@
 
 
 def own_body(rows, cols, comps, groups, slab_ref, before_ref, sent_ref, total_ref):
-    add_own(rows, cols, comps, groups, slab_ref, total_ref, 1)
+    add_own(rows, cols, comps, groups, slab_ref, total_ref, 0)
     sent_ref[...] = before_ref[...] + halves_added(total_ref, rows)
 
 
@@ -800,7 +800,8 @@
     slab1 = along(slab1, 1)
     up = along(up, count_y)
     slab0, down, high, low, pair, before = second_side(model_state, slot_arrays, fold, sea_mask, comps, y_pair)
-    arrived = jnp.concatenate([slab0, slab1, up[:slab_rows], slab3[:slab_rows]])
+    others = jnp.concatenate([slab1, up[:slab_rows], slab3[:slab_rows]])
+    arrived = jnp.concatenate([slab0, others])
     down = along(down, -count_y)
     fars = []
     if y_pair and count_x == 4:
@@ -815,12 +816,15 @@
                 pairs.append(tuple(ends))
             fars.append(lax.ppermute(fold, ("comp", "tx", "ty"), pairs))
 
+    if y_pair:
+        arrived, south, down = lax.optimization_barrier((arrived, south, down))
+        north = south
     other = lax.ppermute(arrived, "comp", [(g, g ^ 2) for g in range(comps)])
 
     sizes = (*model_state.shape[2:], comps, count_x, count_y)
     cut = sizes[0] // 2
     matrices = stencil_matrices(rows, cols)
-    before = scatter_own(arrived, before, rows, cols, comps, slots)
+    before = scatter_own(others, before, rows, cols, comps, slots)
     deep, edge_rows, edge_columns = deep_levels(
         model_state, sea_mask, (up, down, south, north, fold), fars, fold_map,
         wave_speed, diffusivity, surface_gains, matrices, sizes, cut,

time: 35.6 us -> 37.6 us (1.056)
  starting transfers between devices: 7.96 us -> 13.1 us
  waiting for transfers between devices: 4.19 us -> 1.44 us
    ppermute x4, waiting for transfers between devices: 4.05 us -> 0.01 us  [along(): lax.ppermute(block, ('tx', 'ty'), [(s, (s + shift) % positions) for s in...]
    ppermute x1, starting transfers between devices: 0.01 us -> 1.81 us  [shards(): lax.ppermute(jnp.concatenate([pair, slab3[slab_rows:]]), 'ty', [(0, 1), (...]
    ppermute x1, starting transfers between devices: 2.64 us -> 4.4 us  [shards(): came = lax.ppermute(sent, 'comp', [(g, g ^ 1) for g in range(comps)])]
    ppermute x4, starting transfers between devices: 5.24 us -> 6.87 us  [along(): lax.ppermute(block, ('tx', 'ty'), [(s, (s + shift) % positions) for s in...]
    ppermute x1, waiting for transfers between devices: 0.14 us -> 1.42 us  [shards(): lax.ppermute(jnp.concatenate([pair, slab3[slab_rows:]]), 'ty', [(0, 1), (...]
  transfers between devices with their start and end apart: 7 -> 7, of which waited for: 3 -> 1; matrix products, arithmetic and copies ran while one was open for 0% -> 0% of each run, Pallas kernels for 32% -> 29%
where the time goes in v1:
time: 37.6 us; the launch traced here: 37.5 us
  Pallas kernels  22.4 us (60%)
  starting transfers between devices  13.1 us (35%)
  waiting for transfers between devices  1.44 us (4%)
  between operations  0.42 us (1%)
    ppermute x4, starting transfers between devices, along(): lax.ppermute(block, ('tx', 'ty'), [(s, (s + shift) % positions) for s in...  6.87 us
    pallas_call x1, Pallas kernels, scatter_other(): pl.pallas_call(functools.partial(other_body, rows, cols, comps, slots //...  5.34 us
    pallas_call x1, Pallas kernels, first_side(): pl.pallas_call(functools.partial(first_body, levels, rows, cols, comps),...  4.8 us
    ppermute x1, starting transfers between devices, shards(): came = lax.ppermute(sent, 'comp', [(g, g ^ 1) for g in range(comps)])  4.4 us
    pallas_call x1, Pallas kernels, second_side(): pl.pallas_call(functools.partial(second_body, levels, rows, cols, comps,...  3.34 us
    pallas_call x1, Pallas kernels, upper_levels(): pl.pallas_call(functools.partial(upper_body, sizes, end), in_specs=[anywh...  3.07 us
    pallas_call x1, Pallas kernels, deep_levels(): pl.pallas_call(functools.partial(deep_body, sizes, begin), in_specs=[vmem...  2.48 us
    pallas_call x1, Pallas kernels, scatter_own(): pl.pallas_call(functools.partial(own_body, rows, cols, comps, slots // LA...  2.01 us
  transfers between devices with their start and end apart: 7, of which 1 were waited for; matrix products, arithmetic and copies ran while one was open for 0% of the time, Pallas kernels for 29%

profile of v1, /device:TPU:3, one launch (start us, length us, event | category | flops | bytes accessed | tf_op | source)
XLA Modules:
  0.0 37.5 jit_solution(16472646132344962775)
XLA Ops:
  0.0 0.0 copy-start
  0.0 0.0 copy-start.10
  0.0 0.0 copy-start.6
  0.0 0.0 copy-start.5
  0.0 0.0 copy-start.4
  0.0 0.0 copy-start.8
  0.0 4.8 %shard_map.127 = (f32[80,128]{1,0:T(8,128)S(1)}, f32[200,128]{1,0:T(8,128)S(1)}, f32[120,128]{1,0:T(8,128)S(1)}, f32[40,128]{1,0:T(8,128)S(1)}) custom-call(f32[1,4,8,128,256]{4,3,2,1,0:T(8,128)} %state_ref.5, s32[1,1,4,2048]{3,2,1,0:T(4,128)} %own_ref.1, s32[1,1,4,2048]{3,2,1,0:T(4,128)} %target_ref.1, s32[1,1,4,2048]{3,2,1,0:T(4,128)} %ids_ref.1, ...), custom_call_target="tpu_custom_call" | custom-call | tf_op jit(solution)/shard_map/pallas_call | solution.py:268
  4.8 0.0 copy-start.1
  4.9 0.0 copy-start.2
  4.9 0.0 copy-start.3
  4.9 0.0 copy-start.7
  4.9 0.0 copy-start.9
  4.9 0.0 copy-start.11
  4.9 0.0 copy-start.12
  4.9 2.8 %collective-permute-start.2 = (f32[120,128]{1,0:T(8,128)S(1)}, f32[120,128]{1,0:T(8,128)S(1)}, u32[]{:S(2)}, u32[]{:S(2)}) collective-permute-start(f32[120,128]{1,0:T(8,128)S(1)} %get-tuple-element.29), channel_id=1, source_target_pairs={{0,3},{1,4},{2,5},{3,6},{4,7},{5,0},{6,1},{7,2},{8,11},{9,12},{10,... | collective-permute-start | bytes 184328 | tf_op jit(solution)/shard_map/ppermute | solution.py:794
  7.8 0.7 %collective-permute-start = (f32[80,128]{1,0:T(8,128)S(1)}, f32[80,128]{1,0:T(8,128)S(1)}, u32[]{:S(2)}, u32[]{:S(2)}) collective-permute-start(f32[80,128]{1,0:T(8,128)S(1)} %get-tuple-element.27), channel_id=1, source_target_pairs={{0,1},{1,2},{2,3},{3,4},{4,5},{5,6},{6,7},{7,0},{8,9},{9,10},{10,1... | collective-permute-start | bytes 122888 | tf_op jit(solution)/shard_map/ppermute | solution.py:794
  8.5 1.3 %collective-permute-start.1 = (f32[200,128]{1,0:T(8,128)S(1)}, f32[200,128]{1,0:T(8,128)S(1)}, u32[]{:S(2)}, u32[]{:S(2)}) collective-permute-start(f32[200,128]{1,0:T(8,128)S(1)} %get-tuple-element.28), channel_id=1, source_target_pairs={{0,2},{1,3},{2,4},{3,5},{4,6},{5,7},{6,0},{7,1},{8,10},{9,11},{10,... | collective-permute-start | bytes 307208 | tf_op jit(solution)/shard_map/ppermute | solution.py:794
  9.8 0.0 copy-done
  9.8 0.0 copy-done.10
  9.8 0.0 copy-done.6
  9.8 0.0 copy-done.5
  9.8 0.0 copy-done.4
  9.8 0.0 copy-done.8
  9.8 3.3 %shard_map.128 = (f32[80,128]{1,0:T(8,128)S(1)}, f32[120,128]{1,0:T(8,128)S(1)}, f32[40,128]{1,0:T(8,128)}, f32[40,128]{1,0:T(8,128)}, f32[40,128]{1,0:T(8,128)S(1)}, /*index=5*/f32[512,256]{1,0:T(8,128)S(1)}) custom-call(f32[1,4,8,128,256]{4,3,2,1,0:T(8,128)S(1)} %copy-done, s32[1,1,4,2048]{3,2,1,0:T(4,128)S(1)} %copy-done.4, ...), custom_call_target="tpu_custom_call" | custom-call | tf_op jit(solution)/shard_map/pallas_call | solution.py:341
  13.1 2.0 %collective-permute-start.4 = (f32[120,128]{1,0:T(8,128)S(1)}, f32[120,128]{1,0:T(8,128)S(1)}, u32[]{:S(2)}, u32[]{:S(2)}) collective-permute-start(f32[120,128]{1,0:T(8,128)S(1)} %get-tuple-element.31), channel_id=1, source_target_pairs={{0,6},{1,7},{2,0},{3,1},{4,2},{5,3},{6,4},{7,5},{8,14},{9,15},{10,... | collective-permute-start | bytes 184328 | tf_op jit(solution)/shard_map/ppermute | solution.py:794
  15.2 0.0 collective-permute-done.2
  15.2 1.8 %collective-permute-start.3 = (f32[80,128]{1,0:T(8,128)S(1)}, f32[80,128]{1,0:T(8,128)S(1)}, u32[]{:S(2)}, u32[]{:S(2)}) collective-permute-start(f32[80,128]{1,0:T(8,128)S(1)} %pad_maximum_fusion.2), channel_id=1, source_target_pairs={{0,1},{1,0},{2,3},{3,2},{4,5},{5,4},{6,7},{7,6},{8,9},{9,8},{10,11... | collective-permute-start | bytes 122888 | tf_op jit(solution)/shard_map/ppermute | solution.py:808
  17.0 0.0 collective-permute-done.1.up_ref
  17.0 0.0 collective-permute-done
  17.0 0.0 collective-permute-done.4.down_ref
  17.1 1.4 %collective-permute-done.3.south_ref.north_ref = f32[80,128]{1,0:T(8,128)S(1)} collective-permute-done((f32[80,128]{1,0:T(8,128)S(1)}, f32[80,128]{1,0:T(8,128)S(1)}, u32[]{:S(2)}, u32[]{:S(2)}) %collective-permute-start.3) | collective-permute-done | bytes 40992 | tf_op jit(solution)/shard_map/ppermute | solution.py:808
  18.5 0.0 collective-permute-start.5
  18.5 2.0 %shard_map.129.before_ref = f32[512,256]{1,0:T(8,128)S(1)} custom-call(f32[240,128]{1,0:T(8,128)S(1)} %pad_maximum_fusion.1.slab_ref, f32[512,256]{1,0:T(8,128)S(1)} %get-tuple-element.33.before_ref), custom_call_target="tpu_custom_call" | custom-call | tf_op jit(solution)/shard_map/pallas_call | solution.py:732
  20.5 0.0 copy-done.1
  20.5 0.0 copy-done.2
  20.5 0.0 copy-done.3
  20.5 0.0 copy-done.7
  20.6 0.0 copy-done.9
  20.6 0.0 copy-done.11
  20.6 0.0 copy-done.12
  20.6 2.5 %shard_map.130 = (f32[4,4,128,256]{3,2,1,0:T(8,128)S(1)}, f32[2,2,3,8,128]{4,3,2,1,0:T(8,128)S(1)}, bf16[128,256]{1,0:T(8,128)(2,1)S(1)}) custom-call(f32[1,4,8,128,256]{4,3,2,1,0:T(8,128)S(1)} %copy-done, s32[1,128,256]{2,1,0:T(8,128)S(1)} %copy-done.1, f32[200,128]{1,0:T(8,128)S(1)} %collective-permute-done.1.up_ref, ...), custom_call_target="tpu_custom_call" | custom-call | tf_op jit(solution)/shard_map/pallas_call | solution.py:579
  23.1 0.0 collective-permute-done.5.slab_ref
  23.1 5.3 %shard_map.131 = (f32[512,256]{1,0:T(8,128)S(1)}, f32[512,256]{1,0:T(8,128)S(1)}, f32[1,4,8,128,256]{4,3,2,1,0:T(8,128)}) custom-call(f32[320,128]{1,0:T(8,128)S(1)} %collective-permute-done.5.slab_ref, f32[512,256]{1,0:T(8,128)S(1)} %shard_map.129.before_ref, f32[4,4,128,256]{3,2,1,0:T(8,128)S(1)} %get-tuple-element.36.deep_ref), custom_call_target="tpu_custom_call" | custom-call | tf_op jit(solution)/shard_map/pallas_call | solution.py:745
  28.4 4.4 %collective-permute-start.6 = (f32[512,256]{1,0:T(8,128)S(1)}, f32[512,256]{1,0:T(8,128)S(1)}, u32[]{:S(2)}, u32[]{:S(2)}) collective-permute-start(f32[512,256]{1,0:T(8,128)S(1)} %get-tuple-element.44), channel_id=1, source_target_pairs={{0,8},{8,0},{16,24},{24,16},{1,9},{9,1},{17,25},{25,17},{2,10},{10... | collective-permute-start | bytes 1572872 | tf_op jit(solution)/shard_map/ppermute | solution.py:833
  32.8 3.1 %shard_map.132 = (f32[1,4,8,128,256]{4,3,2,1,0:T(8,128)}, f32[3,128,256]{2,1,0:T(8,128)S(1)}, f32[3,128,256]{2,1,0:T(8,128)S(1)}) custom-call(f32[1,4,8,128,256]{4,3,2,1,0:T(8,128)} %get-tuple-element.37.begun_ref, f32[1,4,8,128,256]{4,3,2,1,0:T(8,128)S(1)} %copy-done, s32[1,128,256]{2,1,0:T(8,128)S(1)} %copy-done.1, ...), custom_call_target="tpu_custom_call", output_to_operand_aliasing={{0}: (0, {})} | custom-call | tf_op jit(solution)/shard_map/pallas_call | solution.py:600
  35.9 0.0 collective-permute-done.6.came_ref
  35.9 1.4 %shard_map.133 = f32[1,4,8,128,256]{4,3,2,1,0:T(8,128)} custom-call(f32[1,4,8,128,256]{4,3,2,1,0:T(8,128)} %get-tuple-element.40.state_ref, f32[3,128,256]{2,1,0:T(8,128)S(1)} %get-tuple-element.41.new_ref, f32[3,128,256]{2,1,0:T(8,128)S(1)} %get-tuple-element.42.old_ref, f32[512,256]{1,0:T(8,128)S(1)} %get-tuple-element.43.kept_ref, ...), custom_call_target="tpu_custom_call", output_to_operand_aliasing={{}: (0, {})} | custom-call | tf_op jit(solution)/shard_map/pallas_call | solution.py:772
  (6 shorter events, 0.0 us)
Async XLA Ops:
  0.0 9.8 %copy-start = (f32[1,4,8,128,256]{4,3,2,1,0:T(8,128)S(1)}, f32[1,4,8,128,256]{4,3,2,1,0:T(8,128)}, u32[]{:S(2)}) copy-start(f32[1,4,8,128,256]{4,3,2,1,0:T(8,128)} %state_ref.5) | copy-start | bytes 12582916
  0.0 9.8 %copy-start.10 = (s32[1,1,4]{2,1,0:T(1,128)S(1)}, s32[1,1,4]{2,1,0:T(1,128)}, u32[]{:S(2)}) copy-start(s32[1,1,4]{2,1,0:T(1,128)} %counts_ref.1) | copy-start | bytes 52
  0.0 9.8 %copy-start.6 = (s32[1,1,4,2048]{3,2,1,0:T(4,128)S(1)}, s32[1,1,4,2048]{3,2,1,0:T(4,128)}, u32[]{:S(2)}) copy-start(s32[1,1,4,2048]{3,2,1,0:T(4,128)} %ids_ref.1) | copy-start | bytes 98308
  0.0 9.8 %copy-start.5 = (s32[1,1,4,2048]{3,2,1,0:T(4,128)S(1)}, s32[1,1,4,2048]{3,2,1,0:T(4,128)}, u32[]{:S(2)}) copy-start(s32[1,1,4,2048]{3,2,1,0:T(4,128)} %target_ref.1) | copy-start | bytes 98308
  0.0 9.8 %copy-start.4 = (s32[1,1,4,2048]{3,2,1,0:T(4,128)S(1)}, s32[1,1,4,2048]{3,2,1,0:T(4,128)}, u32[]{:S(2)}) copy-start(s32[1,1,4,2048]{3,2,1,0:T(4,128)} %own_ref.1) | copy-start | bytes 98308
  0.0 9.8 %copy-start.8 = (f32[256]{0:T(256)S(1)}, f32[256]{0:T(256)}, u32[]{:S(2)}) copy-start(f32[256]{0:T(256)} %param.18) | copy-start | bytes 3076
  4.8 15.7 %copy-start.1 = (s32[1,128,256]{2,1,0:T(8,128)S(1)}, s32[1,128,256]{2,1,0:T(8,128)}, u32[]{:S(2)}) copy-start(s32[1,128,256]{2,1,0:T(8,128)} %mask_ref.5) | copy-start | bytes 393220
  4.9 15.7 %copy-start.2 = (bf16[2,512,256]{2,1,0:T(8,128)(2,1)S(1)}, bf16[2,512,256]{2,1,0:T(8,128)(2,1)}, u32[]{:S(2)}) copy-start(bf16[2,512,256]{2,1,0:T(8,128)(2,1)} %constant.5.clone.across_ref) | copy-start | bytes 1572868
  4.9 15.7 %copy-start.3 = (bf16[2,128,256]{2,1,0:T(8,128)(2,1)S(1)}, bf16[2,128,256]{2,1,0:T(8,128)(2,1)}, u32[]{:S(2)}) copy-start(bf16[2,128,256]{2,1,0:T(8,128)(2,1)} %constant.4.clone.along_ref) | copy-start | bytes 393220
  4.9 15.7 %copy-start.7 = (f32[1,3]{1,0:T(1,128)S(1)}, f32[1,3]{1,0:T(1,128)}, u32[]{:S(2)}) copy-start(f32[1,3]{1,0:T(1,128)} %gains_ref.5) | copy-start | bytes 40
  4.9 15.7 %copy-start.9 = (s32[512]{0:T(512)S(1)}, s32[512]{0:T(512)}, u32[]{:S(2)}) copy-start(s32[512]{0:T(512)} %param.23) | copy-start | bytes 6148
  4.9 15.7 %copy-start.11 = (f32[1,8]{1,0:T(1,128)S(1)}, f32[1,8]{1,0:T(1,128)}, u32[]{:S(2)}) copy-start(f32[1,8]{1,0:T(1,128)} %wave_ref.3) | copy-start | bytes 100
  4.9 15.7 %copy-start.12 = (f32[1,8]{1,0:T(1,128)S(1)}, f32[1,8]{1,0:T(1,128)}, u32[]{:S(2)}) copy-start(f32[1,8]{1,0:T(1,128)} %spread_ref.3) | copy-start | bytes 100
  4.9 10.3 %collective-permute-start.2 = (f32[120,128]{1,0:T(8,128)S(1)}, f32[120,128]{1,0:T(8,128)S(1)}, u32[]{:S(2)}, u32[]{:S(2)}) collective-permute-start(f32[120,128]{1,0:T(8,128)S(1)} %get-tuple-element.29), channel_id=1, source_target_pairs={{0,3},{1,4},{2,5},{3,6},{4,7},{5,0},{6,1},{7,2},{8,11},{9,12},{10,... | collective-permute-start | bytes 184328 | tf_op jit(solution)/shard_map/ppermute | solution.py:794
  7.8 9.2 %collective-permute-start = (f32[80,128]{1,0:T(8,128)S(1)}, f32[80,128]{1,0:T(8,128)S(1)}, u32[]{:S(2)}, u32[]{:S(2)}) collective-permute-start(f32[80,128]{1,0:T(8,128)S(1)} %get-tuple-element.27), channel_id=1, source_target_pairs={{0,1},{1,2},{2,3},{3,4},{4,5},{5,6},{6,7},{7,0},{8,9},{9,10},{10,1... | collective-permute-start | bytes 122888 | tf_op jit(solution)/shard_map/ppermute | solution.py:794
  8.5 8.5 %collective-permute-start.1 = (f32[200,128]{1,0:T(8,128)S(1)}, f32[200,128]{1,0:T(8,128)S(1)}, u32[]{:S(2)}, u32[]{:S(2)}) collective-permute-start(f32[200,128]{1,0:T(8,128)S(1)} %get-tuple-element.28), channel_id=1, source_target_pairs={{0,2},{1,3},{2,4},{3,5},{4,6},{5,7},{6,0},{7,1},{8,10},{9,11},{10,... | collective-permute-start | bytes 307208 | tf_op jit(solution)/shard_map/ppermute | solution.py:794
  13.1 3.9 %collective-permute-start.4 = (f32[120,128]{1,0:T(8,128)S(1)}, f32[120,128]{1,0:T(8,128)S(1)}, u32[]{:S(2)}, u32[]{:S(2)}) collective-permute-start(f32[120,128]{1,0:T(8,128)S(1)} %get-tuple-element.31), channel_id=1, source_target_pairs={{0,6},{1,7},{2,0},{3,1},{4,2},{5,3},{6,4},{7,5},{8,14},{9,15},{10,... | collective-permute-start | bytes 184328 | tf_op jit(solution)/shard_map/ppermute | solution.py:794
  15.2 3.3 %collective-permute-start.3 = (f32[80,128]{1,0:T(8,128)S(1)}, f32[80,128]{1,0:T(8,128)S(1)}, u32[]{:S(2)}, u32[]{:S(2)}) collective-permute-start(f32[80,128]{1,0:T(8,128)S(1)} %pad_maximum_fusion.2), channel_id=1, source_target_pairs={{0,1},{1,0},{2,3},{3,2},{4,5},{5,4},{6,7},{7,6},{8,9},{9,8},{10,11... | collective-permute-start | bytes 122888 | tf_op jit(solution)/shard_map/ppermute | solution.py:808
  18.5 4.6 %collective-permute-start.5 = (f32[320,128]{1,0:T(8,128)S(1)}, f32[320,128]{1,0:T(8,128)S(1)}, u32[]{:S(2)}, u32[]{:S(2)}) collective-permute-start(f32[320,128]{1,0:T(8,128)S(1)} %pad_maximum_fusion), channel_id=1, source_target_pairs={{0,16},{8,24},{16,0},{24,8},{1,17},{9,25},{17,1},{25,9},{2,18},{10... | collective-permute-start | bytes 491528 | tf_op jit(solution)/shard_map/ppermute | solution.py:822
  28.4 7.5 %collective-permute-start.6 = (f32[512,256]{1,0:T(8,128)S(1)}, f32[512,256]{1,0:T(8,128)S(1)}, u32[]{:S(2)}, u32[]{:S(2)}) collective-permute-start(f32[512,256]{1,0:T(8,128)S(1)} %get-tuple-element.44), channel_id=1, source_target_pairs={{0,8},{8,0},{16,24},{24,16},{1,9},{9,1},{17,25},{25,17},{2,10},{10... | collective-permute-start | bytes 1572872 | tf_op jit(solution)/shard_map/ppermute | solution.py:833

commit v2 on v1

--- a/solution.py
+++ b/solution.py
@@ -802,6 +802,8 @@
     slab0, down, high, low, pair, before = second_side(model_state, slot_arrays, fold, sea_mask, comps, y_pair)
     others = jnp.concatenate([slab1, up[:slab_rows], slab3[:slab_rows]])
     arrived = jnp.concatenate([slab0, others])
+    other = lax.ppermute(arrived, "comp", [(g, g ^ 2) for g in range(comps)])
+
     down = along(down, -count_y)
     fars = []
     if y_pair and count_x == 4:
@@ -815,11 +817,6 @@
                 ends = [((comps - 1) * count_x + k) * count_y + count_y - 1 for k in ((i + shift) % count_x, i)]
                 pairs.append(tuple(ends))
             fars.append(lax.ppermute(fold, ("comp", "tx", "ty"), pairs))
-
-    if y_pair:
-        arrived, south, down = lax.optimization_barrier((arrived, south, down))
-        north = south
-    other = lax.ppermute(arrived, "comp", [(g, g ^ 2) for g in range(comps)])
 
     sizes = (*model_state.shape[2:], comps, count_x, count_y)
     cut = sizes[0] // 2

time: 37.6 us -> 35.3 us (0.939)
  starting transfers between devices: 13.1 us -> 9.35 us
  waiting for transfers between devices: 1.44 us -> 2.81 us
    ppermute x4, waiting for transfers between devices: 0.01 us -> 2.22 us  [along(): lax.ppermute(block, ('tx', 'ty'), [(s, (s + shift) % positions) for s in...]
    ppermute x1, starting transfers between devices: 4.4 us -> 2.81 us  [shards(): came = lax.ppermute(sent, 'comp', [(g, g ^ 1) for g in range(comps)])]
    ppermute x1, starting transfers between devices: 1.81 us -> 0.3 us  [shards(): lax.ppermute(jnp.concatenate([pair, slab3[slab_rows:]]), 'ty', [(0, 1), (...]
    ppermute x1, waiting for transfers between devices: 1.42 us -> 0.59 us  [shards(): lax.ppermute(jnp.concatenate([pair, slab3[slab_rows:]]), 'ty', [(0, 1), (...]
    ppermute x4, starting transfers between devices: 6.87 us -> 6.17 us  [along(): lax.ppermute(block, ('tx', 'ty'), [(s, (s + shift) % positions) for s in...]
  transfers between devices with their start and end apart: 7 -> 7, of which waited for: 1 -> 2; matrix products, arithmetic and copies ran while one was open for 0% -> 0% of each run, Pallas kernels for 29% -> 31%
where the time goes in v2:
time: 35.3 us; the launch traced here: 35.1 us
  Pallas kernels  22.4 us (63%)
  starting transfers between devices  9.35 us (26%)
  waiting for transfers between devices  2.81 us (8%)
  between operations  0.42 us (1%)
    ppermute x4, starting transfers between devices, along(): lax.ppermute(block, ('tx', 'ty'), [(s, (s + shift) % positions) for s in...  6.17 us
    pallas_call x1, Pallas kernels, scatter_other(): pl.pallas_call(functools.partial(other_body, rows, cols, comps, slots //...  5.34 us
    pallas_call x1, Pallas kernels, first_side(): pl.pallas_call(functools.partial(first_body, levels, rows, cols, comps),...  4.8 us
    pallas_call x1, Pallas kernels, second_side(): pl.pallas_call(functools.partial(second_body, levels, rows, cols, comps,...  3.35 us
    pallas_call x1, Pallas kernels, upper_levels(): pl.pallas_call(functools.partial(upper_body, sizes, end), in_specs=[anywh...  3.07 us
    ppermute x1, starting transfers between devices, shards(): came = lax.ppermute(sent, 'comp', [(g, g ^ 1) for g in range(comps)])  2.81 us
    pallas_call x1, Pallas kernels, deep_levels(): pl.pallas_call(functools.partial(deep_body, sizes, begin), in_specs=[vmem...  2.48 us
    ppermute x4, waiting for transfers between devices, along(): lax.ppermute(block, ('tx', 'ty'), [(s, (s + shift) % positions) for s in...  2.22 us
  transfers between devices with their start and end apart: 7, of which 2 were waited for; matrix products, arithmetic and copies ran while one was open for 0% of the time, Pallas kernels for 31%

profile of v2, /device:TPU:3, one launch (start us, length us, event | category | flops | bytes accessed | tf_op | source)
XLA Modules:
  0.0 35.1 jit_solution(16521387468497129903)
XLA Ops:
  0.0 0.0 copy-start
  0.0 0.0 copy-start.10
  0.0 0.0 copy-start.6
  0.0 0.0 copy-start.5
  0.0 0.0 copy-start.4
  0.0 0.0 copy-start.8
  0.0 4.8 %shard_map.127 = (f32[80,128]{1,0:T(8,128)S(1)}, f32[200,128]{1,0:T(8,128)S(1)}, f32[120,128]{1,0:T(8,128)S(1)}, f32[40,128]{1,0:T(8,128)S(1)}) custom-call(f32[1,4,8,128,256]{4,3,2,1,0:T(8,128)} %state_ref.5, s32[1,1,4,2048]{3,2,1,0:T(4,128)} %own_ref.1, s32[1,1,4,2048]{3,2,1,0:T(4,128)} %target_ref.1, s32[1,1,4,2048]{3,2,1,0:T(4,128)} %ids_ref.1, ...), custom_call_target="tpu_custom_call" | custom-call | tf_op jit(solution)/shard_map/pallas_call | solution.py:268
  4.9 0.0 copy-start.1
  4.9 0.0 copy-start.2
  4.9 0.0 copy-start.3
  4.9 0.0 copy-start.7
  4.9 0.0 copy-start.9
  4.9 0.0 copy-start.11
  4.9 0.0 copy-start.12
  4.9 1.3 %collective-permute-start.1 = (f32[200,128]{1,0:T(8,128)S(1)}, f32[200,128]{1,0:T(8,128)S(1)}, u32[]{:S(2)}, u32[]{:S(2)}) collective-permute-start(f32[200,128]{1,0:T(8,128)S(1)} %get-tuple-element.25), channel_id=1, source_target_pairs={{0,2},{1,3},{2,4},{3,5},{4,6},{5,7},{6,0},{7,1},{8,10},{9,11},{10,... | collective-permute-start | bytes 307208 | tf_op jit(solution)/shard_map/ppermute | solution.py:794
  6.3 2.8 %collective-permute-start.2 = (f32[120,128]{1,0:T(8,128)S(1)}, f32[120,128]{1,0:T(8,128)S(1)}, u32[]{:S(2)}, u32[]{:S(2)}) collective-permute-start(f32[120,128]{1,0:T(8,128)S(1)} %get-tuple-element.26), channel_id=1, source_target_pairs={{0,3},{1,4},{2,5},{3,6},{4,7},{5,0},{6,1},{7,2},{8,11},{9,12},{10,... | collective-permute-start | bytes 184328 | tf_op jit(solution)/shard_map/ppermute | solution.py:794
  9.1 0.7 %collective-permute-start = (f32[80,128]{1,0:T(8,128)S(1)}, f32[80,128]{1,0:T(8,128)S(1)}, u32[]{:S(2)}, u32[]{:S(2)}) collective-permute-start(f32[80,128]{1,0:T(8,128)S(1)} %get-tuple-element.24), channel_id=1, source_target_pairs={{0,1},{1,2},{2,3},{3,4},{4,5},{5,6},{6,7},{7,0},{8,9},{9,10},{10,1... | collective-permute-start | bytes 122888 | tf_op jit(solution)/shard_map/ppermute | solution.py:794
  9.8 0.0 copy-done
  9.8 0.0 copy-done.10
  9.8 0.0 copy-done.6
  9.8 0.0 copy-done.5
  9.8 0.0 copy-done.4
  9.8 0.0 copy-done.8
  9.8 3.3 %shard_map.128 = (f32[80,128]{1,0:T(8,128)S(1)}, f32[120,128]{1,0:T(8,128)S(1)}, f32[40,128]{1,0:T(8,128)}, f32[40,128]{1,0:T(8,128)}, f32[40,128]{1,0:T(8,128)S(1)}, /*index=5*/f32[512,256]{1,0:T(8,128)S(1)}) custom-call(f32[1,4,8,128,256]{4,3,2,1,0:T(8,128)S(1)} %copy-done, s32[1,1,4,2048]{3,2,1,0:T(4,128)S(1)} %copy-done.4, ...), custom_call_target="tpu_custom_call" | custom-call | tf_op jit(solution)/shard_map/pallas_call | solution.py:341
  13.2 1.3 %collective-permute-start.4 = (f32[120,128]{1,0:T(8,128)S(1)}, f32[120,128]{1,0:T(8,128)S(1)}, u32[]{:S(2)}, u32[]{:S(2)}) collective-permute-start(f32[120,128]{1,0:T(8,128)S(1)} %get-tuple-element.28), channel_id=1, source_target_pairs={{0,6},{1,7},{2,0},{3,1},{4,2},{5,3},{6,4},{7,5},{8,14},{9,15},{10,... | collective-permute-start | bytes 184328 | tf_op jit(solution)/shard_map/ppermute | solution.py:794
  14.5 2.2 %collective-permute-done.2 = f32[120,128]{1,0:T(8,128)S(1)} collective-permute-done((f32[120,128]{1,0:T(8,128)S(1)}, f32[120,128]{1,0:T(8,128)S(1)}, u32[]{:S(2)}, u32[]{:S(2)}) %collective-permute-start.2) | collective-permute-done | bytes 61472 | tf_op jit(solution)/shard_map/ppermute | solution.py:794
  16.7 0.0 collective-permute-done.1.up_ref
  16.7 0.0 collective-permute-done
  16.8 0.1 collective-permute-start.3
  16.9 0.3 collective-permute-start.5
  17.2 2.0 %shard_map.129.before_ref = f32[512,256]{1,0:T(8,128)S(1)} custom-call(f32[240,128]{1,0:T(8,128)S(1)} %pad_maximum_fusion.1.slab_ref, f32[512,256]{1,0:T(8,128)S(1)} %get-tuple-element.27.before_ref), custom_call_target="tpu_custom_call" | custom-call | tf_op jit(solution)/shard_map/pallas_call | solution.py:732
  19.2 0.0 collective-permute-done.4.down_ref
  19.2 0.6 %collective-permute-done.5.south_ref.north_ref = f32[80,128]{1,0:T(8,128)S(1)} collective-permute-done((f32[80,128]{1,0:T(8,128)S(1)}, f32[80,128]{1,0:T(8,128)S(1)}, u32[]{:S(2)}, u32[]{:S(2)}) %collective-permute-start.5) | collective-permute-done | bytes 40992 | tf_op jit(solution)/shard_map/ppermute | solution.py:810
  19.8 0.0 copy-done.1
  19.8 0.0 copy-done.2
  19.8 0.0 copy-done.3
  19.8 0.0 copy-done.7
  19.8 0.0 copy-done.9
  19.8 0.0 copy-done.11
  19.8 0.0 copy-done.12
  19.8 2.5 %shard_map.130 = (f32[4,4,128,256]{3,2,1,0:T(8,128)S(1)}, f32[2,2,3,8,128]{4,3,2,1,0:T(8,128)S(1)}, bf16[128,256]{1,0:T(8,128)(2,1)S(1)}) custom-call(f32[1,4,8,128,256]{4,3,2,1,0:T(8,128)S(1)} %copy-done, s32[1,128,256]{2,1,0:T(8,128)S(1)} %copy-done.1, f32[200,128]{1,0:T(8,128)S(1)} %collective-permute-done.1.up_ref, ...), custom_call_target="tpu_custom_call" | custom-call | tf_op jit(solution)/shard_map/pallas_call | solution.py:579
  22.3 0.0 collective-permute-done.3.slab_ref
  22.3 5.3 %shard_map.131 = (f32[512,256]{1,0:T(8,128)S(1)}, f32[512,256]{1,0:T(8,128)S(1)}, f32[1,4,8,128,256]{4,3,2,1,0:T(8,128)}) custom-call(f32[320,128]{1,0:T(8,128)S(1)} %collective-permute-done.3.slab_ref, f32[512,256]{1,0:T(8,128)S(1)} %shard_map.129.before_ref, f32[4,4,128,256]{3,2,1,0:T(8,128)S(1)} %get-tuple-element.30.deep_ref), custom_call_target="tpu_custom_call" | custom-call | tf_op jit(solution)/shard_map/pallas_call | solution.py:745
  27.7 2.8 %collective-permute-start.6 = (f32[512,256]{1,0:T(8,128)S(1)}, f32[512,256]{1,0:T(8,128)S(1)}, u32[]{:S(2)}, u32[]{:S(2)}) collective-permute-start(f32[512,256]{1,0:T(8,128)S(1)} %get-tuple-element.38), channel_id=1, source_target_pairs={{0,8},{8,0},{16,24},{24,16},{1,9},{9,1},{17,25},{25,17},{2,10},{10... | collective-permute-start | bytes 1572872 | tf_op jit(solution)/shard_map/ppermute | solution.py:830
  30.5 3.1 %shard_map.132 = (f32[1,4,8,128,256]{4,3,2,1,0:T(8,128)}, f32[3,128,256]{2,1,0:T(8,128)S(1)}, f32[3,128,256]{2,1,0:T(8,128)S(1)}) custom-call(f32[1,4,8,128,256]{4,3,2,1,0:T(8,128)} %get-tuple-element.31.begun_ref, f32[1,4,8,128,256]{4,3,2,1,0:T(8,128)S(1)} %copy-done, s32[1,128,256]{2,1,0:T(8,128)S(1)} %copy-done.1, ...), custom_call_target="tpu_custom_call", output_to_operand_aliasing={{0}: (0, {})} | custom-call | tf_op jit(solution)/shard_map/pallas_call | solution.py:600
  33.6 0.0 collective-permute-done.6.came_ref
  33.6 1.4 %shard_map.133 = f32[1,4,8,128,256]{4,3,2,1,0:T(8,128)} custom-call(f32[1,4,8,128,256]{4,3,2,1,0:T(8,128)} %get-tuple-element.34.state_ref, f32[3,128,256]{2,1,0:T(8,128)S(1)} %get-tuple-element.35.new_ref, f32[3,128,256]{2,1,0:T(8,128)S(1)} %get-tuple-element.36.old_ref, f32[512,256]{1,0:T(8,128)S(1)} %get-tuple-element.37.kept_ref, ...), custom_call_target="tpu_custom_call", output_to_operand_aliasing={{}: (0, {})} | custom-call | tf_op jit(solution)/shard_map/pallas_call | solution.py:772
  (6 shorter events, 0.0 us)
Async XLA Ops:
  0.0 9.8 %copy-start = (f32[1,4,8,128,256]{4,3,2,1,0:T(8,128)S(1)}, f32[1,4,8,128,256]{4,3,2,1,0:T(8,128)}, u32[]{:S(2)}) copy-start(f32[1,4,8,128,256]{4,3,2,1,0:T(8,128)} %state_ref.5) | copy-start | bytes 12582916
  0.0 9.8 %copy-start.10 = (s32[1,1,4]{2,1,0:T(1,128)S(1)}, s32[1,1,4]{2,1,0:T(1,128)}, u32[]{:S(2)}) copy-start(s32[1,1,4]{2,1,0:T(1,128)} %counts_ref.1) | copy-start | bytes 52
  0.0 9.8 %copy-start.6 = (s32[1,1,4,2048]{3,2,1,0:T(4,128)S(1)}, s32[1,1,4,2048]{3,2,1,0:T(4,128)}, u32[]{:S(2)}) copy-start(s32[1,1,4,2048]{3,2,1,0:T(4,128)} %ids_ref.1) | copy-start | bytes 98308
  0.0 9.8 %copy-start.5 = (s32[1,1,4,2048]{3,2,1,0:T(4,128)S(1)}, s32[1,1,4,2048]{3,2,1,0:T(4,128)}, u32[]{:S(2)}) copy-start(s32[1,1,4,2048]{3,2,1,0:T(4,128)} %target_ref.1) | copy-start | bytes 98308
  0.0 9.8 %copy-start.4 = (s32[1,1,4,2048]{3,2,1,0:T(4,128)S(1)}, s32[1,1,4,2048]{3,2,1,0:T(4,128)}, u32[]{:S(2)}) copy-start(s32[1,1,4,2048]{3,2,1,0:T(4,128)} %own_ref.1) | copy-start | bytes 98308
  0.0 9.8 %copy-start.8 = (f32[256]{0:T(256)S(1)}, f32[256]{0:T(256)}, u32[]{:S(2)}) copy-start(f32[256]{0:T(256)} %param.18) | copy-start | bytes 3076
  4.9 14.9 %copy-start.1 = (s32[1,128,256]{2,1,0:T(8,128)S(1)}, s32[1,128,256]{2,1,0:T(8,128)}, u32[]{:S(2)}) copy-start(s32[1,128,256]{2,1,0:T(8,128)} %mask_ref.5) | copy-start | bytes 393220
  4.9 14.9 %copy-start.2 = (bf16[2,512,256]{2,1,0:T(8,128)(2,1)S(1)}, bf16[2,512,256]{2,1,0:T(8,128)(2,1)}, u32[]{:S(2)}) copy-start(bf16[2,512,256]{2,1,0:T(8,128)(2,1)} %constant.5.clone.across_ref) | copy-start | bytes 1572868
  4.9 14.9 %copy-start.3 = (bf16[2,128,256]{2,1,0:T(8,128)(2,1)S(1)}, bf16[2,128,256]{2,1,0:T(8,128)(2,1)}, u32[]{:S(2)}) copy-start(bf16[2,128,256]{2,1,0:T(8,128)(2,1)} %constant.4.clone.along_ref) | copy-start | bytes 393220
  4.9 14.9 %copy-start.7 = (f32[1,3]{1,0:T(1,128)S(1)}, f32[1,3]{1,0:T(1,128)}, u32[]{:S(2)}) copy-start(f32[1,3]{1,0:T(1,128)} %gains_ref.5) | copy-start | bytes 40
  4.9 14.9 %copy-start.9 = (s32[512]{0:T(512)S(1)}, s32[512]{0:T(512)}, u32[]{:S(2)}) copy-start(s32[512]{0:T(512)} %param.23) | copy-start | bytes 6148
  4.9 14.9 %copy-start.11 = (f32[1,8]{1,0:T(1,128)S(1)}, f32[1,8]{1,0:T(1,128)}, u32[]{:S(2)}) copy-start(f32[1,8]{1,0:T(1,128)} %wave_ref.3) | copy-start | bytes 100
  4.9 14.9 %copy-start.12 = (f32[1,8]{1,0:T(1,128)S(1)}, f32[1,8]{1,0:T(1,128)}, u32[]{:S(2)}) copy-start(f32[1,8]{1,0:T(1,128)} %spread_ref.3) | copy-start | bytes 100
  4.9 11.8 %collective-permute-start.1 = (f32[200,128]{1,0:T(8,128)S(1)}, f32[200,128]{1,0:T(8,128)S(1)}, u32[]{:S(2)}, u32[]{:S(2)}) collective-permute-start(f32[200,128]{1,0:T(8,128)S(1)} %get-tuple-element.25), channel_id=1, source_target_pairs={{0,2},{1,3},{2,4},{3,5},{4,6},{5,7},{6,0},{7,1},{8,10},{9,11},{10,... | collective-permute-start | bytes 307208 | tf_op jit(solution)/shard_map/ppermute | solution.py:794
  6.3 10.4 %collective-permute-start.2 = (f32[120,128]{1,0:T(8,128)S(1)}, f32[120,128]{1,0:T(8,128)S(1)}, u32[]{:S(2)}, u32[]{:S(2)}) collective-permute-start(f32[120,128]{1,0:T(8,128)S(1)} %get-tuple-element.26), channel_id=1, source_target_pairs={{0,3},{1,4},{2,5},{3,6},{4,7},{5,0},{6,1},{7,2},{8,11},{9,12},{10,... | collective-permute-start | bytes 184328 | tf_op jit(solution)/shard_map/ppermute | solution.py:794
  9.1 7.7 %collective-permute-start = (f32[80,128]{1,0:T(8,128)S(1)}, f32[80,128]{1,0:T(8,128)S(1)}, u32[]{:S(2)}, u32[]{:S(2)}) collective-permute-start(f32[80,128]{1,0:T(8,128)S(1)} %get-tuple-element.24), channel_id=1, source_target_pairs={{0,1},{1,2},{2,3},{3,4},{4,5},{5,6},{6,7},{7,0},{8,9},{9,10},{10,1... | collective-permute-start | bytes 122888 | tf_op jit(solution)/shard_map/ppermute | solution.py:794
  13.2 6.0 %collective-permute-start.4 = (f32[120,128]{1,0:T(8,128)S(1)}, f32[120,128]{1,0:T(8,128)S(1)}, u32[]{:S(2)}, u32[]{:S(2)}) collective-permute-start(f32[120,128]{1,0:T(8,128)S(1)} %get-tuple-element.28), channel_id=1, source_target_pairs={{0,6},{1,7},{2,0},{3,1},{4,2},{5,3},{6,4},{7,5},{8,14},{9,15},{10,... | collective-permute-start | bytes 184328 | tf_op jit(solution)/shard_map/ppermute | solution.py:794
  16.8 5.5 %collective-permute-start.3 = (f32[320,128]{1,0:T(8,128)S(1)}, f32[320,128]{1,0:T(8,128)S(1)}, u32[]{:S(2)}, u32[]{:S(2)}) collective-permute-start(f32[320,128]{1,0:T(8,128)S(1)} %pad_maximum_fusion), channel_id=1, source_target_pairs={{0,16},{8,24},{16,0},{24,8},{1,17},{9,25},{17,1},{25,9},{2,18},{10... | collective-permute-start | bytes 491528 | tf_op jit(solution)/shard_map/ppermute | solution.py:805
  16.9 2.9 %collective-permute-start.5 = (f32[80,128]{1,0:T(8,128)S(1)}, f32[80,128]{1,0:T(8,128)S(1)}, u32[]{:S(2)}, u32[]{:S(2)}) collective-permute-start(f32[80,128]{1,0:T(8,128)S(1)} %pad_maximum_fusion.2), channel_id=1, source_target_pairs={{0,1},{1,0},{2,3},{3,2},{4,5},{5,4},{6,7},{7,6},{8,9},{9,8},{10,11... | collective-permute-start | bytes 122888 | tf_op jit(solution)/shard_map/ppermute | solution.py:810
  27.7 5.9 %collective-permute-start.6 = (f32[512,256]{1,0:T(8,128)S(1)}, f32[512,256]{1,0:T(8,128)S(1)}, u32[]{:S(2)}, u32[]{:S(2)}) collective-permute-start(f32[512,256]{1,0:T(8,128)S(1)} %get-tuple-element.38), channel_id=1, source_target_pairs={{0,8},{8,0},{16,24},{24,16},{1,9},{9,1},{17,25},{25,17},{2,10},{10... | collective-permute-start | bytes 1572872 | tf_op jit(solution)/shard_map/ppermute | solution.py:830

commit v3 on v2

--- a/solution.py
+++ b/solution.py
@@ -615,7 +615,7 @@
     lane = iota((1, LANES), 1)
     one = jnp.ones((), BF16)
     zero = jnp.zeros((), BF16)
-    block = 4
+    block = 4 if runs == 1 else DEPTH
 
     def one_chunk(total_ref, chunk):
         n, first, low_slot, high_slot = plan(chunk)

time: 35.3 us -> 35.3 us (level)
  no operation moved by 1% of the time
where the time goes in v3:
time: 35.3 us; the launch traced here: 35.1 us
  Pallas kernels  22.4 us (63%)
  starting transfers between devices  9.35 us (26%)
  waiting for transfers between devices  2.81 us (8%)
  between operations  0.42 us (1%)
    ppermute x4, starting transfers between devices, along(): lax.ppermute(block, ('tx', 'ty'), [(s, (s + shift) % positions) for s in...  6.17 us
    pallas_call x1, Pallas kernels, scatter_other(): pl.pallas_call(functools.partial(other_body, rows, cols, comps, slots //...  5.34 us
    pallas_call x1, Pallas kernels, first_side(): pl.pallas_call(functools.partial(first_body, levels, rows, cols, comps),...  4.8 us
    pallas_call x1, Pallas kernels, second_side(): pl.pallas_call(functools.partial(second_body, levels, rows, cols, comps,...  3.35 us
    pallas_call x1, Pallas kernels, upper_levels(): pl.pallas_call(functools.partial(upper_body, sizes, end), in_specs=[anywh...  3.07 us
    ppermute x1, starting transfers between devices, shards(): came = lax.ppermute(sent, 'comp', [(g, g ^ 1) for g in range(comps)])  2.81 us
    pallas_call x1, Pallas kernels, deep_levels(): pl.pallas_call(functools.partial(deep_body, sizes, begin), in_specs=[vmem...  2.48 us
    ppermute x4, waiting for transfers between devices, along(): lax.ppermute(block, ('tx', 'ty'), [(s, (s + shift) % positions) for s in...  2.22 us
  transfers between devices with their start and end apart: 7, of which 2 were waited for; matrix products, arithmetic and copies ran while one was open for 0% of the time, Pallas kernels for 31%

profile of v3, /device:TPU:3, one launch (start us, length us, event | category | flops | bytes accessed | tf_op | source)
XLA Modules:
  0.0 35.1 jit_solution(16521387468497129903)
XLA Ops:
  0.0 0.0 copy-start
  0.0 0.0 copy-start.10
  0.0 0.0 copy-start.6
  0.0 0.0 copy-start.5
  0.0 0.0 copy-start.4
  0.0 0.0 copy-start.8
  0.0 4.8 %shard_map.127 = (f32[80,128]{1,0:T(8,128)S(1)}, f32[200,128]{1,0:T(8,128)S(1)}, f32[120,128]{1,0:T(8,128)S(1)}, f32[40,128]{1,0:T(8,128)S(1)}) custom-call(f32[1,4,8,128,256]{4,3,2,1,0:T(8,128)} %state_ref.5, s32[1,1,4,2048]{3,2,1,0:T(4,128)} %own_ref.1, s32[1,1,4,2048]{3,2,1,0:T(4,128)} %target_ref.1, s32[1,1,4,2048]{3,2,1,0:T(4,128)} %ids_ref.1, ...), custom_call_target="tpu_custom_call" | custom-call | tf_op jit(solution)/shard_map/pallas_call | solution.py:268
  4.9 0.0 copy-start.1
  4.9 0.0 copy-start.2
  4.9 0.0 copy-start.3
  4.9 0.0 copy-start.7
  4.9 0.0 copy-start.9
  4.9 0.0 copy-start.11
  4.9 0.0 copy-start.12
  4.9 1.3 %collective-permute-start.1 = (f32[200,128]{1,0:T(8,128)S(1)}, f32[200,128]{1,0:T(8,128)S(1)}, u32[]{:S(2)}, u32[]{:S(2)}) collective-permute-start(f32[200,128]{1,0:T(8,128)S(1)} %get-tuple-element.25), channel_id=1, source_target_pairs={{0,2},{1,3},{2,4},{3,5},{4,6},{5,7},{6,0},{7,1},{8,10},{9,11},{10,... | collective-permute-start | bytes 307208 | tf_op jit(solution)/shard_map/ppermute | solution.py:794
  6.3 2.8 %collective-permute-start.2 = (f32[120,128]{1,0:T(8,128)S(1)}, f32[120,128]{1,0:T(8,128)S(1)}, u32[]{:S(2)}, u32[]{:S(2)}) collective-permute-start(f32[120,128]{1,0:T(8,128)S(1)} %get-tuple-element.26), channel_id=1, source_target_pairs={{0,3},{1,4},{2,5},{3,6},{4,7},{5,0},{6,1},{7,2},{8,11},{9,12},{10,... | collective-permute-start | bytes 184328 | tf_op jit(solution)/shard_map/ppermute | solution.py:794
  9.1 0.7 %collective-permute-start = (f32[80,128]{1,0:T(8,128)S(1)}, f32[80,128]{1,0:T(8,128)S(1)}, u32[]{:S(2)}, u32[]{:S(2)}) collective-permute-start(f32[80,128]{1,0:T(8,128)S(1)} %get-tuple-element.24), channel_id=1, source_target_pairs={{0,1},{1,2},{2,3},{3,4},{4,5},{5,6},{6,7},{7,0},{8,9},{9,10},{10,1... | collective-permute-start | bytes 122888 | tf_op jit(solution)/shard_map/ppermute | solution.py:794
  9.8 0.0 copy-done
  9.8 0.0 copy-done.10
  9.8 0.0 copy-done.6
  9.8 0.0 copy-done.5
  9.8 0.0 copy-done.4
  9.8 0.0 copy-done.8
  9.8 3.3 %shard_map.128 = (f32[80,128]{1,0:T(8,128)S(1)}, f32[120,128]{1,0:T(8,128)S(1)}, f32[40,128]{1,0:T(8,128)}, f32[40,128]{1,0:T(8,128)}, f32[40,128]{1,0:T(8,128)S(1)}, /*index=5*/f32[512,256]{1,0:T(8,128)S(1)}) custom-call(f32[1,4,8,128,256]{4,3,2,1,0:T(8,128)S(1)} %copy-done, s32[1,1,4,2048]{3,2,1,0:T(4,128)S(1)} %copy-done.4, ...), custom_call_target="tpu_custom_call" | custom-call | tf_op jit(solution)/shard_map/pallas_call | solution.py:341
  13.2 1.3 %collective-permute-start.4 = (f32[120,128]{1,0:T(8,128)S(1)}, f32[120,128]{1,0:T(8,128)S(1)}, u32[]{:S(2)}, u32[]{:S(2)}) collective-permute-start(f32[120,128]{1,0:T(8,128)S(1)} %get-tuple-element.28), channel_id=1, source_target_pairs={{0,6},{1,7},{2,0},{3,1},{4,2},{5,3},{6,4},{7,5},{8,14},{9,15},{10,... | collective-permute-start | bytes 184328 | tf_op jit(solution)/shard_map/ppermute | solution.py:794
  14.5 2.2 %collective-permute-done.2 = f32[120,128]{1,0:T(8,128)S(1)} collective-permute-done((f32[120,128]{1,0:T(8,128)S(1)}, f32[120,128]{1,0:T(8,128)S(1)}, u32[]{:S(2)}, u32[]{:S(2)}) %collective-permute-start.2) | collective-permute-done | bytes 61472 | tf_op jit(solution)/shard_map/ppermute | solution.py:794
  16.7 0.0 collective-permute-done.1.up_ref
  16.7 0.0 collective-permute-done
  16.8 0.1 collective-permute-start.3
  16.9 0.3 collective-permute-start.5
  17.2 2.0 %shard_map.129.before_ref = f32[512,256]{1,0:T(8,128)S(1)} custom-call(f32[240,128]{1,0:T(8,128)S(1)} %pad_maximum_fusion.1.slab_ref, f32[512,256]{1,0:T(8,128)S(1)} %get-tuple-element.27.before_ref), custom_call_target="tpu_custom_call" | custom-call | tf_op jit(solution)/shard_map/pallas_call | solution.py:732
  19.2 0.0 collective-permute-done.4.down_ref
  19.2 0.6 %collective-permute-done.5.south_ref.north_ref = f32[80,128]{1,0:T(8,128)S(1)} collective-permute-done((f32[80,128]{1,0:T(8,128)S(1)}, f32[80,128]{1,0:T(8,128)S(1)}, u32[]{:S(2)}, u32[]{:S(2)}) %collective-permute-start.5) | collective-permute-done | bytes 40992 | tf_op jit(solution)/shard_map/ppermute | solution.py:810
  19.8 0.0 copy-done.1
  19.8 0.0 copy-done.2
  19.8 0.0 copy-done.3
  19.8 0.0 copy-done.7
  19.8 0.0 copy-done.9
  19.8 0.0 copy-done.11
  19.8 0.0 copy-done.12
  19.8 2.5 %shard_map.130 = (f32[4,4,128,256]{3,2,1,0:T(8,128)S(1)}, f32[2,2,3,8,128]{4,3,2,1,0:T(8,128)S(1)}, bf16[128,256]{1,0:T(8,128)(2,1)S(1)}) custom-call(f32[1,4,8,128,256]{4,3,2,1,0:T(8,128)S(1)} %copy-done, s32[1,128,256]{2,1,0:T(8,128)S(1)} %copy-done.1, f32[200,128]{1,0:T(8,128)S(1)} %collective-permute-done.1.up_ref, ...), custom_call_target="tpu_custom_call" | custom-call | tf_op jit(solution)/shard_map/pallas_call | solution.py:579
  22.3 0.0 collective-permute-done.3.slab_ref
  22.3 5.3 %shard_map.131 = (f32[512,256]{1,0:T(8,128)S(1)}, f32[512,256]{1,0:T(8,128)S(1)}, f32[1,4,8,128,256]{4,3,2,1,0:T(8,128)}) custom-call(f32[320,128]{1,0:T(8,128)S(1)} %collective-permute-done.3.slab_ref, f32[512,256]{1,0:T(8,128)S(1)} %shard_map.129.before_ref, f32[4,4,128,256]{3,2,1,0:T(8,128)S(1)} %get-tuple-element.30.deep_ref), custom_call_target="tpu_custom_call" | custom-call | tf_op jit(solution)/shard_map/pallas_call | solution.py:745
  27.7 2.8 %collective-permute-start.6 = (f32[512,256]{1,0:T(8,128)S(1)}, f32[512,256]{1,0:T(8,128)S(1)}, u32[]{:S(2)}, u32[]{:S(2)}) collective-permute-start(f32[512,256]{1,0:T(8,128)S(1)} %get-tuple-element.38), channel_id=1, source_target_pairs={{0,8},{8,0},{16,24},{24,16},{1,9},{9,1},{17,25},{25,17},{2,10},{10... | collective-permute-start | bytes 1572872 | tf_op jit(solution)/shard_map/ppermute | solution.py:830
  30.5 3.1 %shard_map.132 = (f32[1,4,8,128,256]{4,3,2,1,0:T(8,128)}, f32[3,128,256]{2,1,0:T(8,128)S(1)}, f32[3,128,256]{2,1,0:T(8,128)S(1)}) custom-call(f32[1,4,8,128,256]{4,3,2,1,0:T(8,128)} %get-tuple-element.31.begun_ref, f32[1,4,8,128,256]{4,3,2,1,0:T(8,128)S(1)} %copy-done, s32[1,128,256]{2,1,0:T(8,128)S(1)} %copy-done.1, ...), custom_call_target="tpu_custom_call", output_to_operand_aliasing={{0}: (0, {})} | custom-call | tf_op jit(solution)/shard_map/pallas_call | solution.py:600
  33.6 0.0 collective-permute-done.6.came_ref
  33.6 1.4 %shard_map.133 = f32[1,4,8,128,256]{4,3,2,1,0:T(8,128)} custom-call(f32[1,4,8,128,256]{4,3,2,1,0:T(8,128)} %get-tuple-element.34.state_ref, f32[3,128,256]{2,1,0:T(8,128)S(1)} %get-tuple-element.35.new_ref, f32[3,128,256]{2,1,0:T(8,128)S(1)} %get-tuple-element.36.old_ref, f32[512,256]{1,0:T(8,128)S(1)} %get-tuple-element.37.kept_ref, ...), custom_call_target="tpu_custom_call", output_to_operand_aliasing={{}: (0, {})} | custom-call | tf_op jit(solution)/shard_map/pallas_call | solution.py:772
  (6 shorter events, 0.0 us)
Async XLA Ops:
  0.0 9.8 %copy-start = (f32[1,4,8,128,256]{4,3,2,1,0:T(8,128)S(1)}, f32[1,4,8,128,256]{4,3,2,1,0:T(8,128)}, u32[]{:S(2)}) copy-start(f32[1,4,8,128,256]{4,3,2,1,0:T(8,128)} %state_ref.5) | copy-start | bytes 12582916
  0.0 9.8 %copy-start.10 = (s32[1,1,4]{2,1,0:T(1,128)S(1)}, s32[1,1,4]{2,1,0:T(1,128)}, u32[]{:S(2)}) copy-start(s32[1,1,4]{2,1,0:T(1,128)} %counts_ref.1) | copy-start | bytes 52
  0.0 9.8 %copy-start.6 = (s32[1,1,4,2048]{3,2,1,0:T(4,128)S(1)}, s32[1,1,4,2048]{3,2,1,0:T(4,128)}, u32[]{:S(2)}) copy-start(s32[1,1,4,2048]{3,2,1,0:T(4,128)} %ids_ref.1) | copy-start | bytes 98308
  0.0 9.8 %copy-start.5 = (s32[1,1,4,2048]{3,2,1,0:T(4,128)S(1)}, s32[1,1,4,2048]{3,2,1,0:T(4,128)}, u32[]{:S(2)}) copy-start(s32[1,1,4,2048]{3,2,1,0:T(4,128)} %target_ref.1) | copy-start | bytes 98308
  0.0 9.8 %copy-start.4 = (s32[1,1,4,2048]{3,2,1,0:T(4,128)S(1)}, s32[1,1,4,2048]{3,2,1,0:T(4,128)}, u32[]{:S(2)}) copy-start(s32[1,1,4,2048]{3,2,1,0:T(4,128)} %own_ref.1) | copy-start | bytes 98308
  0.0 9.8 %copy-start.8 = (f32[256]{0:T(256)S(1)}, f32[256]{0:T(256)}, u32[]{:S(2)}) copy-start(f32[256]{0:T(256)} %param.18) | copy-start | bytes 3076
  4.9 14.9 %copy-start.1 = (s32[1,128,256]{2,1,0:T(8,128)S(1)}, s32[1,128,256]{2,1,0:T(8,128)}, u32[]{:S(2)}) copy-start(s32[1,128,256]{2,1,0:T(8,128)} %mask_ref.5) | copy-start | bytes 393220
  4.9 14.9 %copy-start.2 = (bf16[2,512,256]{2,1,0:T(8,128)(2,1)S(1)}, bf16[2,512,256]{2,1,0:T(8,128)(2,1)}, u32[]{:S(2)}) copy-start(bf16[2,512,256]{2,1,0:T(8,128)(2,1)} %constant.5.clone.across_ref) | copy-start | bytes 1572868
  4.9 14.9 %copy-start.3 = (bf16[2,128,256]{2,1,0:T(8,128)(2,1)S(1)}, bf16[2,128,256]{2,1,0:T(8,128)(2,1)}, u32[]{:S(2)}) copy-start(bf16[2,128,256]{2,1,0:T(8,128)(2,1)} %constant.4.clone.along_ref) | copy-start | bytes 393220
  4.9 14.9 %copy-start.7 = (f32[1,3]{1,0:T(1,128)S(1)}, f32[1,3]{1,0:T(1,128)}, u32[]{:S(2)}) copy-start(f32[1,3]{1,0:T(1,128)} %gains_ref.5) | copy-start | bytes 40
  4.9 14.9 %copy-start.9 = (s32[512]{0:T(512)S(1)}, s32[512]{0:T(512)}, u32[]{:S(2)}) copy-start(s32[512]{0:T(512)} %param.23) | copy-start | bytes 6148
  4.9 14.9 %copy-start.11 = (f32[1,8]{1,0:T(1,128)S(1)}, f32[1,8]{1,0:T(1,128)}, u32[]{:S(2)}) copy-start(f32[1,8]{1,0:T(1,128)} %wave_ref.3) | copy-start | bytes 100
  4.9 14.9 %copy-start.12 = (f32[1,8]{1,0:T(1,128)S(1)}, f32[1,8]{1,0:T(1,128)}, u32[]{:S(2)}) copy-start(f32[1,8]{1,0:T(1,128)} %spread_ref.3) | copy-start | bytes 100
  4.9 11.8 %collective-permute-start.1 = (f32[200,128]{1,0:T(8,128)S(1)}, f32[200,128]{1,0:T(8,128)S(1)}, u32[]{:S(2)}, u32[]{:S(2)}) collective-permute-start(f32[200,128]{1,0:T(8,128)S(1)} %get-tuple-element.25), channel_id=1, source_target_pairs={{0,2},{1,3},{2,4},{3,5},{4,6},{5,7},{6,0},{7,1},{8,10},{9,11},{10,... | collective-permute-start | bytes 307208 | tf_op jit(solution)/shard_map/ppermute | solution.py:794
  6.3 10.4 %collective-permute-start.2 = (f32[120,128]{1,0:T(8,128)S(1)}, f32[120,128]{1,0:T(8,128)S(1)}, u32[]{:S(2)}, u32[]{:S(2)}) collective-permute-start(f32[120,128]{1,0:T(8,128)S(1)} %get-tuple-element.26), channel_id=1, source_target_pairs={{0,3},{1,4},{2,5},{3,6},{4,7},{5,0},{6,1},{7,2},{8,11},{9,12},{10,... | collective-permute-start | bytes 184328 | tf_op jit(solution)/shard_map/ppermute | solution.py:794
  9.1 7.7 %collective-permute-start = (f32[80,128]{1,0:T(8,128)S(1)}, f32[80,128]{1,0:T(8,128)S(1)}, u32[]{:S(2)}, u32[]{:S(2)}) collective-permute-start(f32[80,128]{1,0:T(8,128)S(1)} %get-tuple-element.24), channel_id=1, source_target_pairs={{0,1},{1,2},{2,3},{3,4},{4,5},{5,6},{6,7},{7,0},{8,9},{9,10},{10,1... | collective-permute-start | bytes 122888 | tf_op jit(solution)/shard_map/ppermute | solution.py:794
  13.2 6.0 %collective-permute-start.4 = (f32[120,128]{1,0:T(8,128)S(1)}, f32[120,128]{1,0:T(8,128)S(1)}, u32[]{:S(2)}, u32[]{:S(2)}) collective-permute-start(f32[120,128]{1,0:T(8,128)S(1)} %get-tuple-element.28), channel_id=1, source_target_pairs={{0,6},{1,7},{2,0},{3,1},{4,2},{5,3},{6,4},{7,5},{8,14},{9,15},{10,... | collective-permute-start | bytes 184328 | tf_op jit(solution)/shard_map/ppermute | solution.py:794
  16.8 5.5 %collective-permute-start.3 = (f32[320,128]{1,0:T(8,128)S(1)}, f32[320,128]{1,0:T(8,128)S(1)}, u32[]{:S(2)}, u32[]{:S(2)}) collective-permute-start(f32[320,128]{1,0:T(8,128)S(1)} %pad_maximum_fusion), channel_id=1, source_target_pairs={{0,16},{8,24},{16,0},{24,8},{1,17},{9,25},{17,1},{25,9},{2,18},{10... | collective-permute-start | bytes 491528 | tf_op jit(solution)/shard_map/ppermute | solution.py:805
  16.9 2.9 %collective-permute-start.5 = (f32[80,128]{1,0:T(8,128)S(1)}, f32[80,128]{1,0:T(8,128)S(1)}, u32[]{:S(2)}, u32[]{:S(2)}) collective-permute-start(f32[80,128]{1,0:T(8,128)S(1)} %pad_maximum_fusion.2), channel_id=1, source_target_pairs={{0,1},{1,0},{2,3},{3,2},{4,5},{5,4},{6,7},{7,6},{8,9},{9,8},{10,11... | collective-permute-start | bytes 122888 | tf_op jit(solution)/shard_map/ppermute | solution.py:810
  27.7 5.9 %collective-permute-start.6 = (f32[512,256]{1,0:T(8,128)S(1)}, f32[512,256]{1,0:T(8,128)S(1)}, u32[]{:S(2)}, u32[]{:S(2)}) collective-permute-start(f32[512,256]{1,0:T(8,128)S(1)} %get-tuple-element.38), channel_id=1, source_target_pairs={{0,8},{8,0},{16,24},{24,16},{1,9},{9,1},{17,25},{25,17},{2,10},{10... | collective-permute-start | bytes 1572872 | tf_op jit(solution)/shard_map/ppermute | solution.py:830

commit v4 on v2

--- a/solution.py
+++ b/solution.py
@@ -252,7 +252,7 @@
         pltpu.VMEM((6 * rows, cols) if stacked else (3 * rows, 2 * cols), BF16),
         pltpu.VMEM((3, slots // LANES, LANES), I32),
         pltpu.VMEM((slots // LANES, LANES), I32),
-        pltpu.VMEM((3 * slots // LANES * 8, LANES), F32),
+        pltpu.VMEM((3 * slots // LANES * 8 + 8, LANES), F32),
     ]
 
 

time: 35.3 us -> 35.3 us (level)
  no operation moved by 1% of the time
where the time goes in v4:
time: 35.3 us; the launch traced here: 35.1 us
  Pallas kernels  22.4 us (63%)
  starting transfers between devices  9.35 us (26%)
  waiting for transfers between devices  2.82 us (8%)
  between operations  0.42 us (1%)
    ppermute x4, starting transfers between devices, along(): lax.ppermute(block, ('tx', 'ty'), [(s, (s + shift) % positions) for s in...  6.16 us
    pallas_call x1, Pallas kernels, scatter_other(): pl.pallas_call(functools.partial(other_body, rows, cols, comps, slots //...  5.34 us
    pallas_call x1, Pallas kernels, first_side(): pl.pallas_call(functools.partial(first_body, levels, rows, cols, comps),...  4.8 us
    pallas_call x1, Pallas kernels, second_side(): pl.pallas_call(functools.partial(second_body, levels, rows, cols, comps,...  3.36 us
    pallas_call x1, Pallas kernels, upper_levels(): pl.pallas_call(functools.partial(upper_body, sizes, end), in_specs=[anywh...  3.07 us
    ppermute x1, starting transfers between devices, shards(): came = lax.ppermute(sent, 'comp', [(g, g ^ 1) for g in range(comps)])  2.83 us
    pallas_call x1, Pallas kernels, deep_levels(): pl.pallas_call(functools.partial(deep_body, sizes, begin), in_specs=[vmem...  2.48 us
    ppermute x4, waiting for transfers between devices, along(): lax.ppermute(block, ('tx', 'ty'), [(s, (s + shift) % positions) for s in...  2.22 us
  transfers between devices with their start and end apart: 7, of which 2 were waited for; matrix products, arithmetic and copies ran while one was open for 0% of the time, Pallas kernels for 31%

profile of v4, /device:TPU:3, one launch (start us, length us, event | category | flops | bytes accessed | tf_op | source)
XLA Modules:
  0.0 35.1 jit_solution(9722724063714824417)
XLA Ops:
  0.0 0.0 copy-start
  0.0 0.0 copy-start.10
  0.0 0.0 copy-start.6
  0.0 0.0 copy-start.5
  0.0 0.0 copy-start.4
  0.0 0.0 copy-start.8
  0.0 4.8 %shard_map.127 = (f32[80,128]{1,0:T(8,128)S(1)}, f32[200,128]{1,0:T(8,128)S(1)}, f32[120,128]{1,0:T(8,128)S(1)}, f32[40,128]{1,0:T(8,128)S(1)}) custom-call(f32[1,4,8,128,256]{4,3,2,1,0:T(8,128)} %state_ref.5, s32[1,1,4,2048]{3,2,1,0:T(4,128)} %own_ref.1, s32[1,1,4,2048]{3,2,1,0:T(4,128)} %target_ref.1, s32[1,1,4,2048]{3,2,1,0:T(4,128)} %ids_ref.1, ...), custom_call_target="tpu_custom_call" | custom-call | tf_op jit(solution)/shard_map/pallas_call | solution.py:268
  4.8 0.0 copy-start.1
  4.9 0.0 copy-start.2
  4.9 0.0 copy-start.3
  4.9 0.0 copy-start.7
  4.9 0.0 copy-start.9
  4.9 0.0 copy-start.11
  4.9 0.0 copy-start.12
  4.9 1.3 %collective-permute-start.1 = (f32[200,128]{1,0:T(8,128)S(1)}, f32[200,128]{1,0:T(8,128)S(1)}, u32[]{:S(2)}, u32[]{:S(2)}) collective-permute-start(f32[200,128]{1,0:T(8,128)S(1)} %get-tuple-element.25), channel_id=1, source_target_pairs={{0,2},{1,3},{2,4},{3,5},{4,6},{5,7},{6,0},{7,1},{8,10},{9,11},{10,... | collective-permute-start | bytes 307208 | tf_op jit(solution)/shard_map/ppermute | solution.py:794
  6.3 2.8 %collective-permute-start.2 = (f32[120,128]{1,0:T(8,128)S(1)}, f32[120,128]{1,0:T(8,128)S(1)}, u32[]{:S(2)}, u32[]{:S(2)}) collective-permute-start(f32[120,128]{1,0:T(8,128)S(1)} %get-tuple-element.26), channel_id=1, source_target_pairs={{0,3},{1,4},{2,5},{3,6},{4,7},{5,0},{6,1},{7,2},{8,11},{9,12},{10,... | collective-permute-start | bytes 184328 | tf_op jit(solution)/shard_map/ppermute | solution.py:794
  9.1 0.7 %collective-permute-start = (f32[80,128]{1,0:T(8,128)S(1)}, f32[80,128]{1,0:T(8,128)S(1)}, u32[]{:S(2)}, u32[]{:S(2)}) collective-permute-start(f32[80,128]{1,0:T(8,128)S(1)} %get-tuple-element.24), channel_id=1, source_target_pairs={{0,1},{1,2},{2,3},{3,4},{4,5},{5,6},{6,7},{7,0},{8,9},{9,10},{10,1... | collective-permute-start | bytes 122888 | tf_op jit(solution)/shard_map/ppermute | solution.py:794
  9.8 0.0 copy-done
  9.8 0.0 copy-done.10
  9.8 0.0 copy-done.6
  9.8 0.0 copy-done.5
  9.8 0.0 copy-done.4
  9.8 0.0 copy-done.8
  9.8 3.4 %shard_map.128 = (f32[80,128]{1,0:T(8,128)S(1)}, f32[120,128]{1,0:T(8,128)S(1)}, f32[40,128]{1,0:T(8,128)}, f32[40,128]{1,0:T(8,128)}, f32[40,128]{1,0:T(8,128)S(1)}, /*index=5*/f32[512,256]{1,0:T(8,128)S(1)}) custom-call(f32[1,4,8,128,256]{4,3,2,1,0:T(8,128)S(1)} %copy-done, s32[1,1,4,2048]{3,2,1,0:T(4,128)S(1)} %copy-done.4, ...), custom_call_target="tpu_custom_call" | custom-call | tf_op jit(solution)/shard_map/pallas_call | solution.py:341
  13.2 1.3 %collective-permute-start.4 = (f32[120,128]{1,0:T(8,128)S(1)}, f32[120,128]{1,0:T(8,128)S(1)}, u32[]{:S(2)}, u32[]{:S(2)}) collective-permute-start(f32[120,128]{1,0:T(8,128)S(1)} %get-tuple-element.28), channel_id=1, source_target_pairs={{0,6},{1,7},{2,0},{3,1},{4,2},{5,3},{6,4},{7,5},{8,14},{9,15},{10,... | collective-permute-start | bytes 184328 | tf_op jit(solution)/shard_map/ppermute | solution.py:794
  14.5 2.2 %collective-permute-done.2 = f32[120,128]{1,0:T(8,128)S(1)} collective-permute-done((f32[120,128]{1,0:T(8,128)S(1)}, f32[120,128]{1,0:T(8,128)S(1)}, u32[]{:S(2)}, u32[]{:S(2)}) %collective-permute-start.2) | collective-permute-done | bytes 61472 | tf_op jit(solution)/shard_map/ppermute | solution.py:794
  16.7 0.0 collective-permute-done.1.up_ref
  16.7 0.0 collective-permute-done
  16.8 0.1 collective-permute-start.3
  16.9 0.3 collective-permute-start.5
  17.2 2.0 %shard_map.129.before_ref = f32[512,256]{1,0:T(8,128)S(1)} custom-call(f32[240,128]{1,0:T(8,128)S(1)} %pad_maximum_fusion.1.slab_ref, f32[512,256]{1,0:T(8,128)S(1)} %get-tuple-element.27.before_ref), custom_call_target="tpu_custom_call" | custom-call | tf_op jit(solution)/shard_map/pallas_call | solution.py:732
  19.2 0.0 collective-permute-done.4.down_ref
  19.2 0.6 %collective-permute-done.5.south_ref.north_ref = f32[80,128]{1,0:T(8,128)S(1)} collective-permute-done((f32[80,128]{1,0:T(8,128)S(1)}, f32[80,128]{1,0:T(8,128)S(1)}, u32[]{:S(2)}, u32[]{:S(2)}) %collective-permute-start.5) | collective-permute-done | bytes 40992 | tf_op jit(solution)/shard_map/ppermute | solution.py:810
  19.8 0.0 copy-done.1
  19.8 0.0 copy-done.2
  19.8 0.0 copy-done.3
  19.8 0.0 copy-done.7
  19.8 0.0 copy-done.9
  19.8 0.0 copy-done.11
  19.8 0.0 copy-done.12
  19.8 2.5 %shard_map.130 = (f32[4,4,128,256]{3,2,1,0:T(8,128)S(1)}, f32[2,2,3,8,128]{4,3,2,1,0:T(8,128)S(1)}, bf16[128,256]{1,0:T(8,128)(2,1)S(1)}) custom-call(f32[1,4,8,128,256]{4,3,2,1,0:T(8,128)S(1)} %copy-done, s32[1,128,256]{2,1,0:T(8,128)S(1)} %copy-done.1, f32[200,128]{1,0:T(8,128)S(1)} %collective-permute-done.1.up_ref, ...), custom_call_target="tpu_custom_call" | custom-call | tf_op jit(solution)/shard_map/pallas_call | solution.py:579
  22.3 0.0 collective-permute-done.3.slab_ref
  22.3 5.3 %shard_map.131 = (f32[512,256]{1,0:T(8,128)S(1)}, f32[512,256]{1,0:T(8,128)S(1)}, f32[1,4,8,128,256]{4,3,2,1,0:T(8,128)}) custom-call(f32[320,128]{1,0:T(8,128)S(1)} %collective-permute-done.3.slab_ref, f32[512,256]{1,0:T(8,128)S(1)} %shard_map.129.before_ref, f32[4,4,128,256]{3,2,1,0:T(8,128)S(1)} %get-tuple-element.30.deep_ref), custom_call_target="tpu_custom_call" | custom-call | tf_op jit(solution)/shard_map/pallas_call | solution.py:745
  27.7 2.8 %collective-permute-start.6 = (f32[512,256]{1,0:T(8,128)S(1)}, f32[512,256]{1,0:T(8,128)S(1)}, u32[]{:S(2)}, u32[]{:S(2)}) collective-permute-start(f32[512,256]{1,0:T(8,128)S(1)} %get-tuple-element.38), channel_id=1, source_target_pairs={{0,8},{8,0},{16,24},{24,16},{1,9},{9,1},{17,25},{25,17},{2,10},{10... | collective-permute-start | bytes 1572872 | tf_op jit(solution)/shard_map/ppermute | solution.py:830
  30.5 3.1 %shard_map.132 = (f32[1,4,8,128,256]{4,3,2,1,0:T(8,128)}, f32[3,128,256]{2,1,0:T(8,128)S(1)}, f32[3,128,256]{2,1,0:T(8,128)S(1)}) custom-call(f32[1,4,8,128,256]{4,3,2,1,0:T(8,128)} %get-tuple-element.31.begun_ref, f32[1,4,8,128,256]{4,3,2,1,0:T(8,128)S(1)} %copy-done, s32[1,128,256]{2,1,0:T(8,128)S(1)} %copy-done.1, ...), custom_call_target="tpu_custom_call", output_to_operand_aliasing={{0}: (0, {})} | custom-call | tf_op jit(solution)/shard_map/pallas_call | solution.py:600
  33.6 0.0 collective-permute-done.6.came_ref
  33.6 1.4 %shard_map.133 = f32[1,4,8,128,256]{4,3,2,1,0:T(8,128)} custom-call(f32[1,4,8,128,256]{4,3,2,1,0:T(8,128)} %get-tuple-element.34.state_ref, f32[3,128,256]{2,1,0:T(8,128)S(1)} %get-tuple-element.35.new_ref, f32[3,128,256]{2,1,0:T(8,128)S(1)} %get-tuple-element.36.old_ref, f32[512,256]{1,0:T(8,128)S(1)} %get-tuple-element.37.kept_ref, ...), custom_call_target="tpu_custom_call", output_to_operand_aliasing={{}: (0, {})} | custom-call | tf_op jit(solution)/shard_map/pallas_call | solution.py:772
  (6 shorter events, 0.0 us)
Async XLA Ops:
  0.0 9.8 %copy-start = (f32[1,4,8,128,256]{4,3,2,1,0:T(8,128)S(1)}, f32[1,4,8,128,256]{4,3,2,1,0:T(8,128)}, u32[]{:S(2)}) copy-start(f32[1,4,8,128,256]{4,3,2,1,0:T(8,128)} %state_ref.5) | copy-start | bytes 12582916
  0.0 9.8 %copy-start.10 = (s32[1,1,4]{2,1,0:T(1,128)S(1)}, s32[1,1,4]{2,1,0:T(1,128)}, u32[]{:S(2)}) copy-start(s32[1,1,4]{2,1,0:T(1,128)} %counts_ref.1) | copy-start | bytes 52
  0.0 9.8 %copy-start.6 = (s32[1,1,4,2048]{3,2,1,0:T(4,128)S(1)}, s32[1,1,4,2048]{3,2,1,0:T(4,128)}, u32[]{:S(2)}) copy-start(s32[1,1,4,2048]{3,2,1,0:T(4,128)} %ids_ref.1) | copy-start | bytes 98308
  0.0 9.8 %copy-start.5 = (s32[1,1,4,2048]{3,2,1,0:T(4,128)S(1)}, s32[1,1,4,2048]{3,2,1,0:T(4,128)}, u32[]{:S(2)}) copy-start(s32[1,1,4,2048]{3,2,1,0:T(4,128)} %target_ref.1) | copy-start | bytes 98308
  0.0 9.8 %copy-start.4 = (s32[1,1,4,2048]{3,2,1,0:T(4,128)S(1)}, s32[1,1,4,2048]{3,2,1,0:T(4,128)}, u32[]{:S(2)}) copy-start(s32[1,1,4,2048]{3,2,1,0:T(4,128)} %own_ref.1) | copy-start | bytes 98308
  0.0 9.8 %copy-start.8 = (f32[256]{0:T(256)S(1)}, f32[256]{0:T(256)}, u32[]{:S(2)}) copy-start(f32[256]{0:T(256)} %param.18) | copy-start | bytes 3076
  4.8 14.9 %copy-start.1 = (s32[1,128,256]{2,1,0:T(8,128)S(1)}, s32[1,128,256]{2,1,0:T(8,128)}, u32[]{:S(2)}) copy-start(s32[1,128,256]{2,1,0:T(8,128)} %mask_ref.5) | copy-start | bytes 393220
  4.9 14.9 %copy-start.2 = (bf16[2,512,256]{2,1,0:T(8,128)(2,1)S(1)}, bf16[2,512,256]{2,1,0:T(8,128)(2,1)}, u32[]{:S(2)}) copy-start(bf16[2,512,256]{2,1,0:T(8,128)(2,1)} %constant.5.clone.across_ref) | copy-start | bytes 1572868
  4.9 14.9 %copy-start.3 = (bf16[2,128,256]{2,1,0:T(8,128)(2,1)S(1)}, bf16[2,128,256]{2,1,0:T(8,128)(2,1)}, u32[]{:S(2)}) copy-start(bf16[2,128,256]{2,1,0:T(8,128)(2,1)} %constant.4.clone.along_ref) | copy-start | bytes 393220
  4.9 14.9 %copy-start.7 = (f32[1,3]{1,0:T(1,128)S(1)}, f32[1,3]{1,0:T(1,128)}, u32[]{:S(2)}) copy-start(f32[1,3]{1,0:T(1,128)} %gains_ref.5) | copy-start | bytes 40
  4.9 14.9 %copy-start.9 = (s32[512]{0:T(512)S(1)}, s32[512]{0:T(512)}, u32[]{:S(2)}) copy-start(s32[512]{0:T(512)} %param.23) | copy-start | bytes 6148
  4.9 14.9 %copy-start.11 = (f32[1,8]{1,0:T(1,128)S(1)}, f32[1,8]{1,0:T(1,128)}, u32[]{:S(2)}) copy-start(f32[1,8]{1,0:T(1,128)} %wave_ref.3) | copy-start | bytes 100
  4.9 14.9 %copy-start.12 = (f32[1,8]{1,0:T(1,128)S(1)}, f32[1,8]{1,0:T(1,128)}, u32[]{:S(2)}) copy-start(f32[1,8]{1,0:T(1,128)} %spread_ref.3) | copy-start | bytes 100
  4.9 11.8 %collective-permute-start.1 = (f32[200,128]{1,0:T(8,128)S(1)}, f32[200,128]{1,0:T(8,128)S(1)}, u32[]{:S(2)}, u32[]{:S(2)}) collective-permute-start(f32[200,128]{1,0:T(8,128)S(1)} %get-tuple-element.25), channel_id=1, source_target_pairs={{0,2},{1,3},{2,4},{3,5},{4,6},{5,7},{6,0},{7,1},{8,10},{9,11},{10,... | collective-permute-start | bytes 307208 | tf_op jit(solution)/shard_map/ppermute | solution.py:794
  6.3 10.4 %collective-permute-start.2 = (f32[120,128]{1,0:T(8,128)S(1)}, f32[120,128]{1,0:T(8,128)S(1)}, u32[]{:S(2)}, u32[]{:S(2)}) collective-permute-start(f32[120,128]{1,0:T(8,128)S(1)} %get-tuple-element.26), channel_id=1, source_target_pairs={{0,3},{1,4},{2,5},{3,6},{4,7},{5,0},{6,1},{7,2},{8,11},{9,12},{10,... | collective-permute-start | bytes 184328 | tf_op jit(solution)/shard_map/ppermute | solution.py:794
  9.1 7.7 %collective-permute-start = (f32[80,128]{1,0:T(8,128)S(1)}, f32[80,128]{1,0:T(8,128)S(1)}, u32[]{:S(2)}, u32[]{:S(2)}) collective-permute-start(f32[80,128]{1,0:T(8,128)S(1)} %get-tuple-element.24), channel_id=1, source_target_pairs={{0,1},{1,2},{2,3},{3,4},{4,5},{5,6},{6,7},{7,0},{8,9},{9,10},{10,1... | collective-permute-start | bytes 122888 | tf_op jit(solution)/shard_map/ppermute | solution.py:794
  13.2 6.0 %collective-permute-start.4 = (f32[120,128]{1,0:T(8,128)S(1)}, f32[120,128]{1,0:T(8,128)S(1)}, u32[]{:S(2)}, u32[]{:S(2)}) collective-permute-start(f32[120,128]{1,0:T(8,128)S(1)} %get-tuple-element.28), channel_id=1, source_target_pairs={{0,6},{1,7},{2,0},{3,1},{4,2},{5,3},{6,4},{7,5},{8,14},{9,15},{10,... | collective-permute-start | bytes 184328 | tf_op jit(solution)/shard_map/ppermute | solution.py:794
  16.8 5.5 %collective-permute-start.3 = (f32[320,128]{1,0:T(8,128)S(1)}, f32[320,128]{1,0:T(8,128)S(1)}, u32[]{:S(2)}, u32[]{:S(2)}) collective-permute-start(f32[320,128]{1,0:T(8,128)S(1)} %pad_maximum_fusion), channel_id=1, source_target_pairs={{0,16},{8,24},{16,0},{24,8},{1,17},{9,25},{17,1},{25,9},{2,18},{10... | collective-permute-start | bytes 491528 | tf_op jit(solution)/shard_map/ppermute | solution.py:805
  16.9 2.9 %collective-permute-start.5 = (f32[80,128]{1,0:T(8,128)S(1)}, f32[80,128]{1,0:T(8,128)S(1)}, u32[]{:S(2)}, u32[]{:S(2)}) collective-permute-start(f32[80,128]{1,0:T(8,128)S(1)} %pad_maximum_fusion.2), channel_id=1, source_target_pairs={{0,1},{1,0},{2,3},{3,2},{4,5},{5,4},{6,7},{7,6},{8,9},{9,8},{10,11... | collective-permute-start | bytes 122888 | tf_op jit(solution)/shard_map/ppermute | solution.py:810
  27.7 5.9 %collective-permute-start.6 = (f32[512,256]{1,0:T(8,128)S(1)}, f32[512,256]{1,0:T(8,128)S(1)}, u32[]{:S(2)}, u32[]{:S(2)}) collective-permute-start(f32[512,256]{1,0:T(8,128)S(1)} %get-tuple-element.38), channel_id=1, source_target_pairs={{0,8},{8,0},{16,24},{24,16},{1,9},{9,1},{17,25},{25,17},{2,10},{10... | collective-permute-start | bytes 1572872 | tf_op jit(solution)/shard_map/ppermute | solution.py:830
